TPU v7x, 32 devices: a whole 2x2x4 slice. The times are simulated.
32 devices in a mesh: grp: 2 (over x), gx: 16 (over z, y, core).
Axes of the slice: x: 2, y: 2, z: 4, core: 2. Of those that a mesh axis runs over, the one named last changes fastest.
Arguments:
- point_fraction: bfloat16 [512, 3, 128], P(('grp', 'gx')), parts along dimension 0, may hold values from 0 to 1
- point_features: bfloat16 [512, 8, 128], P(('grp', 'gx')), parts along dimension 0, may hold values from -6 to 6
- base_cell: int32 [512, 128], P(('grp', 'gx')), parts along dimension 0, may hold values from 0 to 3966, as said below
- corner_bits: int32 [512, 128], P(('grp', 'gx')), parts along dimension 0, may hold values from 0 to 255
- owner_map: int32 [512, 1], P(('grp', 'gx')), parts along dimension 0, may hold values from 0 to 15; in each aligned block of 16 rows (0 to 15, 16 to 31, ...) at most 2 rows name the same one
- cotangent: bfloat16 [512, 4, 128], P(('grp', 'gx')), parts along dimension 0, may hold values from -6 to 6
- lift_weight: bfloat16 [64, 8], replicated, may hold values from -2 to 2
- encode_inner: float32 [64, 3], replicated, may hold values from -6 to 6
- encode_bias: float32 [64], replicated, may hold values from -4 to 4
- encode_outer: bfloat16 [64, 64], replicated, may hold values from -0.75 to 0.75
- stencil_weight: bfloat16 [27, 64, 64], replicated, may hold values from -0.15625 to 0.15625
- stencil_bias: float32 [64], replicated, may hold values from -3 to 3
- decode_inner: float32 [64, 3], replicated, may hold values from -6 to 6
- decode_bias: float32 [64], replicated, may hold values from -4 to 4
- decode_outer: bfloat16 [64, 64], replicated, may hold values from -0.75 to 0.75
- output_weight: bfloat16 [4, 64], replicated, may hold values from -0.75 to 0.75
Outputs:
- predictions: bfloat16 [512, 4, 128], P(('grp', 'gx')), parts along dimension 0
- stencil_grad: float32 [128, 1728], P(('grp', 'gx')), parts along dimension 0
There are 2 independent parts, one for each index of `grp`. A program takes and returns all parts, laid end to end along the dimension named above; an argument that names none is the same for every part. Nothing has to cross between parts.
Inputs may be any that keep to these rules, and one draw needn't show every extreme that they name: `base_cell`: flat index x * 16 * 128 + y * 128 + z with x < 2, y < 15, z < 127. `corner_bits`: bit j marks corner j of the point's cell as within the radius. `owner_map`: among the blocks of one device at most 2 have the same owner; some device has exactly 2 blocks with one owner.
All inputs are finite; a program needn't handle non-finite values.
Results may differ from a plain program's by a relative error of at most 0.02.
Values may be sent and summed in bfloat16 or wider, within the bound.
A program may use at most 64 MiB of HBM per device.

v0:
```python
import jax
import jax.numpy as jnp
from jax import lax
from jax.sharding import PartitionSpec as P

CAP = 2
GXD = 2
GY = 16
GZ = 128


def passed_along(block, axis, distance):
    devices = range(lax.axis_size(axis))
    route = [(i - distance, i) for i in devices if i - distance in devices]
    return lax.ppermute(block, axis, route)


def extended_2(block, sides, width):
    for axis, dim in sides:
        count = lax.axis_size(axis)
        forward = [(i, i + 1) for i in range(count - 1)]
        backward = [(target, source) for source, target in forward]
        low = lax.ppermute(
            lax.slice_in_dim(block, block.shape[dim] - width, None, axis=dim), axis, forward
        )
        high = lax.ppermute(lax.slice_in_dim(block, 0, width, axis=dim), axis, backward)
        block = jnp.concatenate([low, block, high], axis=dim)
    return block


def smooth(values):
    return (
        0.5
        * values
        * (1.0 + jnp.tanh(0.7978845608 * (values + 0.044715 * values * values * values)))
    )


def smooth_slope(values):
    return jax.jvp(smooth, (values,), (jnp.ones_like(values),))[1]


def corner_table():
    corner = jnp.arange(8, dtype=jnp.int32)
    return jnp.stack([corner // 4, corner // 2 % 2, corner % 2])


def corner_offsets():
    shifts = corner_table()
    return shifts[0] * (GY * GZ) + shifts[1] * GZ + shifts[2]


def corner_live(bit_words):
    corner = jnp.arange(8, dtype=jnp.int32)
    return (jnp.right_shift(bit_words[None], corner[:, None, None]) & 1).astype(jnp.float32)


def kernel_values(fraction, first_layer, offset_bias, second_layer):
    shifts = corner_table().astype(jnp.float32)
    placed = jnp.transpose(fraction.astype(jnp.float32), (1, 0, 2))
    displace = shifts[:, :, None, None] - placed[:, None]
    hidden_pre = (
        first_layer[:, 0, None, None, None] * displace[0]
        + first_layer[:, 1, None, None, None] * displace[1]
        + first_layer[:, 2, None, None, None] * displace[2]
        + offset_bias[:, None, None, None]
    )
    hidden = smooth(hidden_pre).astype(jnp.bfloat16)
    return jnp.einsum(
        "ck,kjgp->cjgp", second_layer, hidden, preferred_element_type=jnp.float32
    ).astype(jnp.bfloat16)


def lift_points(lift_weight, features):
    return jnp.einsum(
        "cf,gfp->cgp", lift_weight, features, preferred_element_type=jnp.float32
    ).astype(jnp.bfloat16)


def spread(grid_sum, kernel_out, values, corner_on, cell_ids):
    contribution = (
        kernel_out.astype(jnp.float32) * values.astype(jnp.float32)[:, None] * corner_on[None]
    )
    return grid_sum.at[:, cell_ids.reshape(-1)].add(contribution.reshape(grid_sum.shape[0], -1))


def stencil(source, weight, offset_bias, planes):
    padded = jnp.pad(source, ((0, 0), (0, 0), (1, 1), (1, 1)))
    running = jnp.zeros((source.shape[0], planes, GY, GZ), jnp.float32)
    for offset in range(27):
        along_x, along_y, along_z = (offset // 9, offset // 3 % 3, offset % 3)
        window = padded[
            :, along_x : along_x + planes, along_y : along_y + GY, along_z : along_z + GZ
        ]
        running = running + jnp.einsum(
            "oc,cxyz->oxyz", weight[offset], window, preferred_element_type=jnp.float32
        )
    return running + offset_bias[:, None, None, None]


def stencil_terms(grad_pre, source, planes):
    padded = jnp.pad(source, ((0, 0), (0, 0), (1, 1), (1, 1)))
    partial_terms = []
    for offset in range(27):
        along_x, along_y, along_z = (offset // 9, offset // 3 % 3, offset % 3)
        window = padded[
            :, along_x : along_x + planes, along_y : along_y + GY, along_z : along_z + GZ
        ]
        partial_terms.append(
            jnp.einsum("oxyz,cxyz->oc", grad_pre, window, preferred_element_type=jnp.float32)
        )
    stacked = jnp.stack(partial_terms, axis=1)
    return stacked.reshape(stacked.shape[0], -1)


def settle(grad_sum):
    grid_view = grad_sum.reshape(grad_sum.shape[0], GXD + 1, GY, GZ)
    arriving = passed_along(grid_view[:, GXD].astype(jnp.bfloat16), "gx", 1).astype(jnp.float32)
    return grid_view[:, :GXD].at[:, 0].add(arriving)


def shards(
    point_fraction,
    point_features,
    base_cell,
    corner_bits,
    owner_map,
    cotangent,
    lift_weight,
    encode_inner,
    encode_bias,
    encode_outer,
    stencil_weight,
    stencil_bias,
    decode_inner,
    decode_bias,
    decode_outer,
    output_weight,
):
    devices = lax.axis_size("gx")
    slot_count = devices * CAP
    channels = lift_weight.shape[0]
    target = owner_map[:, 0]
    blocks_held = target.shape[0]
    matching = target[:, None] == target[None, :]
    earlier = jnp.arange(blocks_held)[None, :] < jnp.arange(blocks_held)[:, None]
    ranking = jnp.sum(jnp.logical_and(matching, earlier), axis=1)
    places = target * CAP + ranking

    def to_slots(values):
        return jnp.zeros((slot_count,) + values.shape[1:], values.dtype).at[places].set(values)

    fraction_in, features_in, cotangent_in = (
        lax.all_to_all(to_slots(point_fraction), "gx", split_axis=0, concat_axis=0, tiled=True),
        lax.all_to_all(to_slots(point_features), "gx", split_axis=0, concat_axis=0, tiled=True),
        lax.all_to_all(to_slots(cotangent), "gx", split_axis=0, concat_axis=0, tiled=True),
    )
    base_in, bits_in = (
        lax.all_to_all(to_slots(base_cell), "gx", split_axis=0, concat_axis=0, tiled=True),
        lax.all_to_all(to_slots(corner_bits), "gx", split_axis=0, concat_axis=0, tiled=True),
    )
    rounds = slot_count // 8
    offsets = corner_offsets()
    extended = (GXD + 1) * GY * GZ

    def grouped(values):
        return values.reshape((rounds, 8) + values.shape[1:])

    portions = (
        grouped(fraction_in),
        grouped(features_in),
        grouped(base_in),
        grouped(bits_in),
        grouped(cotangent_in),
    )
    empty_grid = jnp.zeros((channels, extended), jnp.float32)

    def encode_common(grid_sum, portion):
        fraction, features, base_ids, bit_words, unused = portion
        kernel_out = kernel_values(fraction, encode_inner, encode_bias, encode_outer)
        lifted = lift_points(lift_weight, features)
        corner_on = corner_live(bit_words)
        cell_ids = base_ids[None] + offsets[:, None, None]
        return (spread(grid_sum, kernel_out, lifted, corner_on, cell_ids), corner_on, cell_ids)

    def backward_query(cotangent_part):
        return jnp.einsum(
            "oc,gop->cgp", output_weight, cotangent_part, preferred_element_type=jnp.float32
        ).astype(jnp.bfloat16)

    def encode_only(grid_sum, portion):
        grid_sum, corner_on, cell_ids = encode_common(grid_sum, portion)
        return (grid_sum, None)

    grid_sum, unused = lax.scan(encode_only, empty_grid, portions)
    grid_view = grid_sum.reshape(channels, GXD + 1, GY, GZ)
    edge_sum = passed_along(grid_view[:, GXD].astype(jnp.bfloat16), "gx", 1).astype(jnp.float32)
    latent_in = grid_view[:, :GXD].at[:, 0].add(edge_sum).astype(jnp.bfloat16)
    faced = extended_2(latent_in, (("gx", 1),), 1)
    stencil_pre = stencil(faced, stencil_weight, stencil_bias, GXD)
    latent_out = smooth(stencil_pre).astype(jnp.bfloat16)
    beyond = passed_along(latent_out[:, 0], "gx", -1)
    latent_ext = jnp.concatenate([latent_out, beyond[:, None]], axis=1)
    latent_flat = latent_ext.reshape(channels, -1)

    def query_points(kernel_out, corner_on, cell_ids):
        gathered = jnp.take(latent_flat, cell_ids.reshape(-1), axis=1).reshape(kernel_out.shape)
        queried = jnp.sum(
            kernel_out.astype(jnp.float32) * gathered.astype(jnp.float32) * corner_on[None], axis=1
        ).astype(jnp.bfloat16)
        return jnp.einsum(
            "oc,cgp->gop", output_weight, queried, preferred_element_type=jnp.float32
        ).astype(jnp.bfloat16)

    def decode_step(grad_sum, portion):
        fraction, features, base_ids, bit_words, cotangent_part = portion
        kernel_out = kernel_values(fraction, decode_inner, decode_bias, decode_outer)
        corner_on = corner_live(bit_words)
        cell_ids = base_ids[None] + offsets[:, None, None]
        predicted = query_points(kernel_out, corner_on, cell_ids)
        grad_sum = spread(grad_sum, kernel_out, backward_query(cotangent_part), corner_on, cell_ids)
        return (grad_sum, predicted)

    grad_sum, predicted = lax.scan(decode_step, empty_grid, portions)
    grad_out = settle(grad_sum)
    grad_pre = (grad_out * smooth_slope(stencil_pre)).astype(jnp.bfloat16)
    partial_terms = stencil_terms(grad_pre, faced, GXD)
    stencil_grad = lax.psum_scatter(partial_terms, "gx", scatter_dimension=0, tiled=True)
    returned = lax.all_to_all(
        predicted.reshape((slot_count,) + predicted.shape[2:]),
        "gx",
        split_axis=0,
        concat_axis=0,
        tiled=True,
    )
    return (returned[places], stencil_grad)


def solution(mesh):
    return jax.shard_map(
        shards,
        mesh=mesh,
        in_specs=(
            P(("grp", "gx"), None, None),
            P(("grp", "gx"), None, None),
            P(("grp", "gx"), None),
            P(("grp", "gx"), None),
            P(("grp", "gx"), None),
            P(("grp", "gx"), None, None),
            P(),
            P(),
            P(),
            P(),
            P(),
            P(),
            P(),
            P(),
            P(),
            P(),
        ),
        out_specs=(P(("grp", "gx"), None, None), P(("grp", "gx"), None)),
        check_vma=False,
    )
```

profile of v0, /device:TPU:0, one launch (start us, length us, event | category | flops | bytes accessed | tf_op | source)
XLA Modules:
  0.0 865.1 jit_solution(1721028049638441438)
XLA Ops:
  10.1 7.4 all-to-all-start
  18.9 5.1 all-to-all-done
  24.0 3.5 all-to-all-start.3
  40.2 3.8 all-to-all-done.1
  44.1 3.5 all-to-all-start.4
  47.6 6.8 all-to-all-done.4
  54.7 250.0 %while.32 = (s32[]{:T(128)}, f32[64,6144]{0,1:T(8,128)S(1)}, s32[4,8,128]{2,1,0:T(8,128)S(1)}, f32[64,3]{0,1:T(4,128)S(1)}, bf16[4,8,3,128]{3,1,2,0:T(8,128)(2,1...) while((s32[]{:T(128)}, f32[64,6144]{0,1:T(8,128)S(1)}, ...), condition=%wide.region_8.9_spmd.clone, body=%wide.region_6.8_spmd.clone.sunk | while | flops 78859848 | bytes 22170680 | solution.py:195
  60.5 3.8 copy.172
  64.4 53.1 %scatter_fusion = f32[64,6144]{0,1:T(8,128)S(1)} fusion(f32[64,6144]{0,1:T(8,128)S(1)} %get-tuple-element.786, s32[8192]{0:T(1024)S(1)} %bitcast.713, f32[8192,64]{1,0:T(8,128)} %copy.172), kind=kCustom, calls=%fused_computation.2.clone.clone.1 | custom fusion | flops 524288 | bytes 6324224 | tf_op jit(solution)/shard_map/while/body/eval_jaxpr/scatter-add | solution.py:84
  123.3 3.8 copy.172
  127.2 55.0 %scatter_fusion = f32[64,6144]{0,1:T(8,128)S(1)} fusion(f32[64,6144]{0,1:T(8,128)S(1)} %get-tuple-element.786, s32[8192]{0:T(1024)S(1)} %bitcast.713, f32[8192,64]{1,0:T(8,128)} %copy.172), kind=kCustom, calls=%fused_computation.2.clone.clone.1 | custom fusion | flops 524288 | bytes 6324224 | tf_op jit(solution)/shard_map/while/body/eval_jaxpr/scatter-add | solution.py:84
  188.0 3.8 copy.172
  191.9 51.5 %scatter_fusion = f32[64,6144]{0,1:T(8,128)S(1)} fusion(f32[64,6144]{0,1:T(8,128)S(1)} %get-tuple-element.786, s32[8192]{0:T(1024)S(1)} %bitcast.713, f32[8192,64]{1,0:T(8,128)} %copy.172), kind=kCustom, calls=%fused_computation.2.clone.clone.1 | custom fusion | flops 524288 | bytes 6324224 | tf_op jit(solution)/shard_map/while/body/eval_jaxpr/scatter-add | solution.py:84
  249.2 3.8 copy.172
  253.1 51.5 %scatter_fusion = f32[64,6144]{0,1:T(8,128)S(1)} fusion(f32[64,6144]{0,1:T(8,128)S(1)} %get-tuple-element.786, s32[8192]{0:T(1024)S(1)} %bitcast.713, f32[8192,64]{1,0:T(8,128)} %copy.172), kind=kCustom, calls=%fused_computation.2.clone.clone.1 | custom fusion | flops 524288 | bytes 6324224 | tf_op jit(solution)/shard_map/while/body/eval_jaxpr/scatter-add | solution.py:84
  338.6 11.0 %all-to-all-start.2 = ((bf16[32,4,128]{2,1,0:T(4,128)(2,1)}), bf16[32,4,128]{2,1,0:T(4,128)(2,1)S(1)}, u32[]{:S(2)}, u32[]{:S(2)}) async-start(bf16[32,4,128]{2,1,0:T(4,128)(2,1)} %scatter_fusion.3), calls=%async_computation.2 | async-start | bytes 65536 | tf_op jit(solution)/shard_map/all_to_all | solution.py:156
  351.5 4.7 all-to-all-done.2
  356.5 389.4 %while.33 = (s32[]{:T(128)}, f32[64,6144]{0,1:T(8,128)S(1)}, bf16[4,8,4,128]{3,2,1,0:T(4,128)(2,1)}, s32[4,8,128]{2,1,0:T(8,128)S(1)}, f32[64,3]{0,1:T(4,128)S(1...) while((s32[]{:T(128)}, f32[64,6144]{0,1:T(8,128)S(1)}, ...), condition=%wide.region_12.13_spmd.clone, body=%wide.region_9.12_spmd.clone.sunk | while | flops 81485384 | bytes 27794536 | solution.py:224
  356.7 29.8 %gather_fusion = bf16[8192,64]{1,0:T(8,128)(2,1)} fusion(bf16[64,6144]{0,1:T(8,128)(2,1)} %get-tuple-element.844, s32[8192]{0:T(1024)S(1)} %broadcast_clamp_fusion.2), kind=kCustom, calls=%fused_computation.clone.clone.1 | custom fusion | bytes 2129920 | tf_op jit(solution)/shard_map/while/body/eval_jaxpr/jit(_take)/gather | solution.py:207
  396.6 3.8 copy.176
  400.4 53.1 %scatter_fusion.1 = f32[64,6144]{0,1:T(8,128)S(1)} fusion(f32[64,6144]{0,1:T(8,128)S(1)} %get-tuple-element.821, s32[8192]{0:T(1024)S(1)} %bitcast.712, f32[8192,64]{1,0:T(8,128)} %copy.176), kind=kCustom, calls=%fused_computation.3.clone.clone.1 | custom fusion | flops 524288 | bytes 6324224 | tf_op jit(solution)/shard_map/while/body/eval_jaxpr/scatter-add | solution.py:84
  454.4 29.8 %gather_fusion = bf16[8192,64]{1,0:T(8,128)(2,1)} fusion(bf16[64,6144]{0,1:T(8,128)(2,1)} %get-tuple-element.844, s32[8192]{0:T(1024)S(1)} %broadcast_clamp_fusion.2), kind=kCustom, calls=%fused_computation.clone.clone.1 | custom fusion | bytes 2129920 | tf_op jit(solution)/shard_map/while/body/eval_jaxpr/jit(_take)/gather | solution.py:207
  494.3 3.8 copy.176
  498.0 55.0 %scatter_fusion.1 = f32[64,6144]{0,1:T(8,128)S(1)} fusion(f32[64,6144]{0,1:T(8,128)S(1)} %get-tuple-element.821, s32[8192]{0:T(1024)S(1)} %bitcast.712, f32[8192,64]{1,0:T(8,128)} %copy.176), kind=kCustom, calls=%fused_computation.3.clone.clone.1 | custom fusion | flops 524288 | bytes 6324224 | tf_op jit(solution)/shard_map/while/body/eval_jaxpr/scatter-add | solution.py:84
  553.9 29.8 %gather_fusion = bf16[8192,64]{1,0:T(8,128)(2,1)} fusion(bf16[64,6144]{0,1:T(8,128)(2,1)} %get-tuple-element.844, s32[8192]{0:T(1024)S(1)} %broadcast_clamp_fusion.2), kind=kCustom, calls=%fused_computation.clone.clone.1 | custom fusion | bytes 2129920 | tf_op jit(solution)/shard_map/while/body/eval_jaxpr/jit(_take)/gather | solution.py:207
  593.8 3.8 copy.176
  597.6 51.5 %scatter_fusion.1 = f32[64,6144]{0,1:T(8,128)S(1)} fusion(f32[64,6144]{0,1:T(8,128)S(1)} %get-tuple-element.821, s32[8192]{0:T(1024)S(1)} %bitcast.712, f32[8192,64]{1,0:T(8,128)} %copy.176), kind=kCustom, calls=%fused_computation.3.clone.clone.1 | custom fusion | flops 524288 | bytes 6324224 | tf_op jit(solution)/shard_map/while/body/eval_jaxpr/scatter-add | solution.py:84
  650.0 29.8 %gather_fusion = bf16[8192,64]{1,0:T(8,128)(2,1)} fusion(bf16[64,6144]{0,1:T(8,128)(2,1)} %get-tuple-element.844, s32[8192]{0:T(1024)S(1)} %broadcast_clamp_fusion.2), kind=kCustom, calls=%fused_computation.clone.clone.1 | custom fusion | bytes 2129920 | tf_op jit(solution)/shard_map/while/body/eval_jaxpr/jit(_take)/gather | solution.py:207
  689.9 3.8 copy.176
  693.7 51.5 %scatter_fusion.1 = f32[64,6144]{0,1:T(8,128)S(1)} fusion(f32[64,6144]{0,1:T(8,128)S(1)} %get-tuple-element.821, s32[8192]{0:T(1024)S(1)} %bitcast.712, f32[8192,64]{1,0:T(8,128)} %copy.176), kind=kCustom, calls=%fused_computation.3.clone.clone.1 | custom fusion | flops 524288 | bytes 6324224 | tf_op jit(solution)/shard_map/while/body/eval_jaxpr/scatter-add | solution.py:84
  773.9 6.6 all-to-all-done.5
  781.7 74.7 %all-reduce.4.cloned.1.call-done = f32[64,1728]{1,0:T(8,128)} async-done(((f32[64,1728]{1,0:T(8,128)}), f32[64,1728]{1,0:T(8,128)}) %all-reduce.4.cloned.1.call-update) | async-done | bytes 442384
  (299 shorter events, 149.6 us)
Async XLA Ops:
  7.2 47.5 %copy-start.12 = (bf16[64,8]{0,1:T(8,128)(2,1)S(1)}, bf16[64,8]{0,1:T(8,128)(2,1)}, u32[]{:S(2)}) copy-start(bf16[64,8]{0,1:T(8,128)(2,1)} %param.30) | copy-start | bytes 3076
  7.2 47.5 %copy-start.13 = (f32[64,3]{0,1:T(4,128)S(1)}, f32[64,3]{0,1:T(4,128)}, u32[]{:S(2)}) copy-start(f32[64,3]{0,1:T(4,128)} %param.31) | copy-start | bytes 2308
  7.2 47.5 %copy-start.19 = (f32[64]{0:T(128)S(1)}, f32[64]{0:T(128)}, u32[]{:S(2)}) copy-start(f32[64]{0:T(128)} %param.32) | copy-start | bytes 772
  7.2 47.5 %copy-start.17 = (bf16[64,64]{1,0:T(8,128)(2,1)S(1)}, bf16[64,64]{1,0:T(8,128)(2,1)}, u32[]{:S(2)}) copy-start(bf16[64,64]{1,0:T(8,128)(2,1)} %param.33) | copy-start | bytes 24580
  10.1 13.9 %all-to-all-start = ((s32[16,2,128]{2,1,0:T(2,128)}), s32[16,2,128]{2,1,0:T(2,128)S(1)}, u32[]{:S(2)}, u32[]{:S(2)}) async-start(s32[16,2,128]{2,1,0:T(2,128)} %bitcast.3), calls=%async_computation | async-start | bytes 32768 | tf_op jit(solution)/shard_map/all_to_all | solution.py:159
  24.0 10.0 %all-to-all-start.3 = ((s32[16,2,128]{2,1,0:T(2,128)}), s32[16,2,128]{2,1,0:T(2,128)S(1)}, u32[]{:S(2)}, u32[]{:S(2)}) async-start(s32[16,2,128]{2,1,0:T(2,128)} %bitcast.7), calls=%async_computation.3 | async-start | bytes 32768 | tf_op jit(solution)/shard_map/all_to_all | solution.py:160
  34.0 10.1 %all-to-all-start.1 = ((bf16[32,3,128]{2,1,0:T(4,128)(2,1)}), bf16[32,3,128]{2,1,0:T(4,128)(2,1)S(1)}, u32[]{:S(2)}, u32[]{:S(2)}) async-start(bf16[32,3,128]{2,1,0:T(4,128)(2,1)} %scatter_fusion.2), calls=%async_computation.1 | async-start | bytes 65536 | tf_op jit(solution)/shard_map/all_to_all | solution.py:154
  44.1 10.4 %all-to-all-start.4 = ((bf16[32,8,128]{2,1,0:T(8,128)(2,1)}), bf16[32,8,128]{2,1,0:T(8,128)(2,1)S(1)}, u32[]{:S(2)}, u32[]{:S(2)}) async-start(bf16[32,8,128]{2,1,0:T(8,128)(2,1)} %scatter_fusion.4), calls=%async_computation.4 | async-start | bytes 131072 | tf_op jit(solution)/shard_map/all_to_all | solution.py:155
  307.5 7.4 collective-permute-start
  313.3 6.5 copy-start.10
  316.0 16.1 %copy-start.2 = (bf16[64,2,16,128]{3,0,2,1:T(8,128)(2,1)}, bf16[64,2,16,128]{3,0,2,1:T(8,128)(2,1)S(1)}, u32[]{:S(2)}) copy-start(bf16[64,2,16,128]{3,0,2,1:T(8,128)(2,1)S(1)} %fusion.152) | copy-start | bytes 1572868
  316.0 4.0 collective-permute-start.1
  318.3 3.6 collective-permute-start.2
  320.1 10.6 %copy-start.8 = (bf16[64,1,16,128]{3,0,2,1:T(8,128)(2,1)}, bf16[64,1,16,128]{3,0,2,1:T(8,128)(2,1)S(1)}, u32[]{:S(2)}) copy-start(bf16[64,1,16,128]{3,0,2,1:T(8,128)(2,1)S(1)} %collective-permute-done.1) | copy-start | bytes 786436
  321.9 10.1 %copy-start.6 = (bf16[64,1,16,128]{3,0,2,1:T(8,128)(2,1)}, bf16[64,1,16,128]{3,0,2,1:T(8,128)(2,1)S(1)}, u32[]{:S(2)}) copy-start(bf16[64,1,16,128]{3,0,2,1:T(8,128)(2,1)S(1)} %collective-permute-done.2) | copy-start | bytes 786436
  323.3 9.0 %copy-start = (bf16[64,4,18,130]{3,0,2,1:T(8,128)(2,1)}, bf16[64,4,18,130]{3,0,2,1:T(8,128)(2,1)S(1)}, u32[]{:S(2)}) copy-start(bf16[64,4,18,130]{3,0,2,1:T(8,128)(2,1)S(1)} %select_maximum_fusion) | copy-start | bytes 3594244
  332.3 4.2 copy-start.15
  334.6 15.3 %collective-permute-start.3 = (bf16[64,16,128]{2,0,1:T(8,128)(2,1)S(1)}, bf16[64,16,128]{2,0,1:T(8,128)(2,1)S(1)}, u32[]{:S(2)}, u32[]{:S(2)}) collective-permute-start(bf16[64,16,128]{2,0,1:T(8,128)(2,1)S(1)} %slice_bitcast_fusion.12), channel_id=1, source_target_pairs={{1,0},{2,1},{3,2},{4,3},{5,4},{6,5},{7,6},{8,7},{9,8},{10,9},{11,1... | collective-permute-start | bytes 786440 | tf_op jit(solution)/shard_map/ppermute | solution.py:15
  338.6 17.6 %all-to-all-start.2 = ((bf16[32,4,128]{2,1,0:T(4,128)(2,1)}), bf16[32,4,128]{2,1,0:T(4,128)(2,1)S(1)}, u32[]{:S(2)}, u32[]{:S(2)}) async-start(bf16[32,4,128]{2,1,0:T(4,128)(2,1)} %scatter_fusion.3), calls=%async_computation.2 | async-start | bytes 65536 | tf_op jit(solution)/shard_map/all_to_all | solution.py:156
  349.6 506.8 %all-reduce.4.cloned.1.call-start = ((), (), s32[]{:S(2)}) async-start(), calls=%async_computation.6 | async-start | bytes 917504
  350.0 6.5 copy-start.11
  350.0 6.5 copy-start.14
  350.0 6.5 copy-start.18
  350.0 6.5 copy-start.20
  748.0 8.2 collective-permute-start.4
  752.8 2.3 copy-start.4
  752.8 4.8 copy-start.5
  756.3 2.1 copy-start.1
  758.3 1.3 copy-start.3
  758.4 1.3 copy-start.9
  767.1 2.1 copy-start.21
  770.4 10.1 %all-to-all-start.5 = ((bf16[32,4,128]{2,1,0:T(4,128)(2,1)}), bf16[32,4,128]{2,1,0:T(4,128)(2,1)S(1)}, u32[]{:S(2)}, u32[]{:S(2)}) async-start(bf16[32,4,128]{2,1,0:T(4,128)(2,1)} %bitcast.108), calls=%async_computation.5 | async-start | bytes 65536 | tf_op jit(solution)/shard_map/all_to_all | solution.py:229
  (2 other events, 2.7 us)
Sparse Core Ops, SparseCore 0:
  769.3 87.0 all-reduce.3
where the time goes:
time: 875 us; the launch traced here: 865 us
  other arithmetic  431 us (49%)
  local copies, waits for them, and re-layouts  225 us (26%)
  waiting for transfers between devices  107 us (12%)
  matrix products  43.7 us (5%)
  starting transfers between devices  41.8 us (5%)
  between operations  16 us (2%)
    scatter-add x8, other arithmetic, spread(): grid_sum.at[:, cell_ids.reshape(-1)]  422 us
    gather x8, local copies, waits for them, and re-layouts, query_points(): jnp.take(latent_flat, cell_ids.reshape(-1), axis=1)  130 us
    unnamed x2, waiting for transfers between devices  74.7 us
    reshape x8, local copies, waits for them, and re-layouts, spread(): contribution.reshape(grid_sum.shape[0], -1)  30.3 us
    while x8, local copies, waits for them, and re-layouts  20.6 us
    dot_general x8, matrix products, kernel_values(): jnp.einsum('ck,kjgp->cjgp', second_layer, hidden, preferred_element_type=...  18.7 us
  transfers between devices with their start and end apart: 12, of which 8 were waited for; matrix products, arithmetic and copies ran while one was open for 3% of the time, Pallas kernels for 0%

commit v1 on v0

v1 whole, which is shorter than its diff:
```python
import functools

import jax
import jax.numpy as jnp
from jax import lax
from jax.experimental import pallas as pl
from jax.experimental.pallas import tpu as pltpu
from jax.sharding import PartitionSpec as P

CAP = 2
GXD = 2
GY = 16
GZ = 128
PLANE = GY * GZ
BASE = GXD * PLANE
EXT = (GXD + 1) * PLANE
PADDED = (GY + 2) * GZ
GROUP = 4
CHUNK = GROUP * 128
TILE = 256
BF = jnp.bfloat16
F32 = jnp.float32
NT = (((1,), (1,)), ((), ()))
VMEM_LIMIT = 56 * 1024 * 1024


def smooth(v):
    return 0.5 * v * (1.0 + jnp.tanh(v * (0.7978845608 + (0.7978845608 * 0.044715) * (v * v))))


def smooth_slope(v):
    square = v * v
    t = jnp.tanh(v * (0.7978845608 + (0.7978845608 * 0.044715) * square))
    inner = 0.7978845608 + (3.0 * 0.7978845608 * 0.044715) * square
    return 0.5 * (1.0 + t) + 0.5 * v * (1.0 - t * t) * inner


def point_chunk(order_ref, pts_ref, chunk):
    return jnp.concatenate(
        [pts_ref[order_ref[chunk * GROUP + q]] for q in range(GROUP)], axis=1
    )


def cells_of(points):
    return (points[16:17] * GZ + points[17:18]).astype(jnp.int32)


def scatter_kernel(keep, order_ref, count_ref, pts_ref, value_w_ref, inner_ref, bias_ref, outer_ref, *rest):
    if keep:
        grid_ref, kept_ref, acc_ref, part_ref = rest
    else:
        grid_ref, acc_ref, part_ref = rest
    channels = outer_ref.shape[0]
    chunks = (count_ref[0] + (GROUP - 1)) // GROUP
    acc_ref[...] = jnp.zeros_like(acc_ref)
    inner = inner_ref[...]

    @pl.loop(0, chunks)
    def _(chunk):
        points = point_chunk(order_ref, pts_ref, chunk)
        values = jnp.dot(value_w_ref[...], points.astype(BF), preferred_element_type=F32)
        values = values.astype(BF).astype(F32)
        cell = cells_of(points)
        bits = points[18:19].astype(jnp.int32)
        base = bias_ref[...] - (
            inner[:, 0:1] * points[12:13] + inner[:, 1:2] * points[13:14] + inner[:, 2:3] * points[14:15]
        )
        for j in range(8):
            shift = inner[:, 0:1] * (j // 4) + inner[:, 1:2] * (j // 2 % 2) + inner[:, 2:3] * (j % 2)
            hidden = smooth(base + shift).astype(BF)
            out = jnp.dot(outer_ref[...], hidden, preferred_element_type=F32)
            live = ((bits >> j) & 1).astype(F32)
            out = (out * live).astype(BF)
            if keep:
                kept_ref[chunk, j * channels : (j + 1) * channels, :] = out
            part_ref[j * channels : (j + 1) * channels, :] = (out.astype(F32) * values).astype(BF)

        @pl.loop(0, BASE // TILE)
        def _(t):
            start = pl.multiple_of(t * TILE, TILE)
            ids = lax.broadcasted_iota(jnp.int32, (TILE, CHUNK), 0) + start
            hot = jnp.where(ids == cell, 1.0, 0.0).astype(BF)
            acc_ref[:, pl.ds(start, TILE)] += lax.dot_general(
                part_ref[...], hot, NT, preferred_element_type=F32
            )

    for row in range((GXD + 1) * GY):
        halves = [None, None]
        for j in range(8):
            source = row - (j // 4) * GY - j // 2 % 2
            if 0 <= source < GXD * GY:
                piece = acc_ref[j * channels : (j + 1) * channels, source * GZ : (source + 1) * GZ]
                have = halves[j % 2]
                halves[j % 2] = piece if have is None else have + piece
        total = halves[0] + pltpu.roll(halves[1], 1, 1)
        grid_ref[:, row * GZ : (row + 1) * GZ] = total.astype(grid_ref.dtype)


def scatter_points(order, count, pts, value_w, inner, bias, outer, keep):
    channels = outer.shape[0]
    slots = pts.shape[0]
    smem = pl.BlockSpec(memory_space=pltpu.SMEM)
    vmem = pl.BlockSpec(memory_space=pltpu.VMEM)
    shapes = [jax.ShapeDtypeStruct((channels, EXT), F32 if keep else BF)]
    if keep:
        shapes.append(jax.ShapeDtypeStruct((slots // GROUP, 8 * channels, CHUNK), BF))
    return pl.pallas_call(
        functools.partial(scatter_kernel, keep),
        out_shape=shapes,
        in_specs=[smem, smem] + [vmem] * 5,
        out_specs=[vmem] * len(shapes),
        scratch_shapes=[
            pltpu.VMEM((8 * channels, BASE), F32),
            pltpu.VMEM((8 * channels, CHUNK), BF),
        ],
        compiler_params=pltpu.CompilerParams(vmem_limit_bytes=VMEM_LIMIT),
        cost_estimate=pl.CostEstimate(
            flops=2 * 8 * channels * BASE * slots * 64, bytes_accessed=4 << 20, transcendentals=0
        ),
    )(order, count, pts, value_w, inner, bias, outer)


def level_kernel(
    order_ref, count_ref, edge_ref, pts_ref, own_ref, left_ref, right_ref, grad_ref, kept_ref,
    weight_ref, bias_ref, out_w_ref, pred_ref, sg_ref, lz_ref, pre_ref, lat_ref, l8_ref, hot_ref,
    gp_ref, win_ref, sum_ref,
):
    channels = own_ref.shape[0]
    inside = jnp.where(edge_ref[0] > 0, 0.0, 1.0).astype(F32)
    z = lax.broadcasted_iota(jnp.int32, (channels, PLANE), 1) % GZ
    first, last = z == 0, z == GZ - 1
    lz_ref[...] = jnp.zeros_like(lz_ref)

    def put_plane(index, plane):
        start = index * PADDED + GZ
        lz_ref[channels : 2 * channels, start : start + PLANE] = plane.astype(BF)
        below = jnp.where(first, 0.0, pltpu.roll(plane, 1, 1))
        above = jnp.where(last, 0.0, pltpu.roll(plane, PLANE - 1, 1))
        lz_ref[0:channels, start : start + PLANE] = below.astype(BF)
        lz_ref[2 * channels :, start : start + PLANE] = above.astype(BF)

    def own(k):
        return own_ref[:, k * PLANE : (k + 1) * PLANE].astype(F32)

    put_plane(0, left_ref[:, 0:PLANE].astype(F32))
    put_plane(1, own(0) + left_ref[:, PLANE:].astype(F32))
    put_plane(2, own(1))
    put_plane(3, (own(2) + right_ref[:, 0:PLANE].astype(F32)) * inside)
    put_plane(4, right_ref[:, PLANE:].astype(F32))

    for x in range(3):
        total = None
        for a in range(3):
            start = (x + a) * PADDED
            terms = jnp.dot(
                weight_ref[a * 3 * channels : (a + 1) * 3 * channels, :],
                lz_ref[:, start : start + PADDED],
                preferred_element_type=F32,
            )
            for e in range(3):
                piece = terms[e * channels : (e + 1) * channels, e * GZ : e * GZ + PLANE]
                total = piece if total is None else total + piece
        pre = total + bias_ref[...]
        pre_ref[x] = pre
        out = smooth(pre)
        if x == 2:
            out = out * inside
        lat_ref[0, :, x * PLANE : (x + 1) * PLANE] = out.astype(BF)
        lat_ref[1, :, x * PLANE : (x + 1) * PLANE] = pltpu.roll(out, PLANE - 1, 1).astype(BF)
    lat_ref[:, :, 3 * PLANE :] = jnp.zeros((2, channels, GZ), BF)
    for j in range(8):
        start = (j // 4) * PLANE + (j // 2 % 2) * GZ
        l8_ref[j * channels : (j + 1) * channels, :] = lat_ref[j % 2, :, start : start + BASE]

    pred_ref[...] = jnp.zeros_like(pred_ref)
    chunks = (count_ref[0] + (GROUP - 1)) // GROUP

    @pl.loop(0, chunks)
    def _(chunk):
        cell = cells_of(point_chunk(order_ref, pts_ref, chunk))

        @pl.loop(0, BASE // TILE)
        def _(t):
            start = pl.multiple_of(t * TILE, TILE)
            ids = lax.broadcasted_iota(jnp.int32, (TILE, CHUNK), 0) + start
            hot_ref[pl.ds(start, TILE), :] = jnp.where(ids == cell, 1.0, 0.0).astype(BF)

        queried = None
        for j in range(8):
            rows = slice(j * channels, (j + 1) * channels)
            if j % 4 == 0:
                wide = jnp.dot(
                    l8_ref[j * channels : (j + 4) * channels, :], hot_ref[...], preferred_element_type=F32
                )
            got = wide[(j % 4) * channels : (j % 4 + 1) * channels]
            term = got * kept_ref[chunk, rows, :].astype(F32)
            queried = term if queried is None else queried + term
        predicted = jnp.dot(out_w_ref[...], queried.astype(BF), preferred_element_type=F32)
        for q in range(GROUP):
            pred_ref[order_ref[chunk * GROUP + q]] = predicted[:, q * 128 : (q + 1) * 128]

    for x in range(3):
        grad = grad_ref[:, x * PLANE : (x + 1) * PLANE] * smooth_slope(pre_ref[x])
        if x == 2:
            grad = grad * inside
        gp_ref[0:channels, :] = jnp.where(last, 0.0, pltpu.roll(grad, PLANE - 1, 1)).astype(BF)
        gp_ref[channels : 2 * channels, :] = grad.astype(BF)
        gp_ref[2 * channels :, :] = jnp.where(first, 0.0, pltpu.roll(grad, 1, 1)).astype(BF)
        for k in range(9):
            start = (x + k // 3) * PADDED + (k % 3) * GZ
            win_ref[k * channels : (k + 1) * channels, :] = lz_ref[
                channels : 2 * channels, start : start + PLANE
            ]
        term = lax.dot_general(gp_ref[...], win_ref[...], NT, preferred_element_type=F32)
        if x == 0:
            sum_ref[...] = term
        else:
            sum_ref[...] += term
    for k in range(27):
        f, place = k % 3, k // 3
        sg_ref[:, k * channels : (k + 1) * channels] = sum_ref[
            f * channels : (f + 1) * channels, place * channels : (place + 1) * channels
        ].astype(BF)


def level(order, count, edge, pts, own, left, right, grad, kept, weight, bias, out_w):
    channels = own.shape[0]
    slots = pts.shape[0]
    smem = pl.BlockSpec(memory_space=pltpu.SMEM)
    vmem = pl.BlockSpec(memory_space=pltpu.VMEM)
    return pl.pallas_call(
        level_kernel,
        out_shape=[
            jax.ShapeDtypeStruct((slots, out_w.shape[0], 128), F32),
            jax.ShapeDtypeStruct((channels, 27 * channels), BF),
        ],
        in_specs=[smem] * 3 + [vmem] * 9,
        out_specs=[vmem] * 2,
        scratch_shapes=[
            pltpu.VMEM((3 * channels, 5 * PADDED), BF),
            pltpu.VMEM((3, channels, PLANE), F32),
            pltpu.VMEM((2, channels, EXT + GZ), BF),
            pltpu.VMEM((8 * channels, BASE), BF),
            pltpu.VMEM((BASE, CHUNK), BF),
            pltpu.VMEM((3 * channels, PLANE), BF),
            pltpu.VMEM((9 * channels, PLANE), BF),
            pltpu.VMEM((3 * channels, 9 * channels), F32),
        ],
        compiler_params=pltpu.CompilerParams(vmem_limit_bytes=VMEM_LIMIT),
    )(order, count, edge, pts, own, left, right, grad, kept, weight, bias, out_w)


def shards(
    point_fraction, point_features, base_cell, corner_bits, owner_map, cotangent, lift_weight,
    encode_inner, encode_bias, encode_outer, stencil_weight, stencil_bias, decode_inner,
    decode_bias, decode_outer, output_weight,
):
    devices = lax.axis_size("gx")
    me = lax.axis_index("gx")
    slots = devices * CAP
    channels = lift_weight.shape[0]
    target = owner_map[:, 0]
    held = target.shape[0]
    matching = target[:, None] == target[None, :]
    earlier = jnp.arange(held)[None, :] < jnp.arange(held)[:, None]
    ranking = jnp.sum(jnp.logical_and(matching, earlier), axis=1)
    places = target * CAP + ranking
    pick = (places[:, None] == jnp.arange(slots)[None, :]).astype(BF)

    packed = jnp.concatenate(
        [
            point_features,
            cotangent,
            point_fraction,
            jnp.zeros((held, 1, 128), BF),
            (base_cell // GZ).astype(BF)[:, None],
            (base_cell % GZ).astype(BF)[:, None],
            corner_bits.astype(BF)[:, None],
            jnp.ones((held, 1, 128), BF),
            jnp.zeros((held, 4, 128), BF),
        ],
        axis=1,
    ).reshape(held, -1)
    sent = jnp.dot(pick.T, packed, preferred_element_type=F32).astype(BF)
    pts = lax.all_to_all(sent, "gx", split_axis=0, concat_axis=0, tiled=True)
    pts = pts.reshape(slots, 24, 128).astype(F32)

    active = pts[:, 19, 0] > 0.5
    before = jnp.arange(slots)[None, :] < jnp.arange(slots)[:, None]
    count = jnp.sum(active.astype(jnp.int32))
    ahead_on = jnp.sum((before & active[None, :]).astype(jnp.int32), axis=1)
    ahead_off = jnp.sum((before & ~active[None, :]).astype(jnp.int32), axis=1)
    place = jnp.where(active, ahead_on, count + ahead_off)
    order = jnp.sum(
        jnp.where(place[None, :] == jnp.arange(slots)[:, None], jnp.arange(slots)[None, :], 0), axis=1
    ).astype(jnp.int32)
    count = count.reshape(1)
    edge = (me == devices - 1).astype(jnp.int32).reshape(1)

    lift24 = jnp.pad(lift_weight, ((0, 0), (0, 24 - lift_weight.shape[1])))
    query24 = jnp.pad(output_weight.T, ((0, 0), (8, 12)))
    (own,) = scatter_points(
        order, count, pts, lift24, encode_inner, encode_bias[:, None], encode_outer, False
    )
    up = [(i, i + 1) for i in range(devices - 1)]
    down = [(i + 1, i) for i in range(devices - 1)]
    left = lax.ppermute(own[:, PLANE:], "gx", up)
    right = lax.ppermute(own[:, :BASE], "gx", down)
    grad, kept = scatter_points(
        order, count, pts, query24, decode_inner, decode_bias[:, None], decode_outer, True
    )
    weight = (
        stencil_weight.reshape(9, 3, channels, channels)
        .transpose(0, 2, 1, 3)
        .reshape(9 * channels, 3 * channels)
    )
    out_w = jnp.pad(output_weight, ((0, 4), (0, 0)))
    predicted, terms = level(
        order, count, edge, pts, own, left, right, grad, kept, weight, stencil_bias[:, None], out_w
    )
    outc = output_weight.shape[0]
    predicted = predicted[:, :outc].astype(BF).reshape(devices, -1)
    payload = jnp.concatenate([predicted, terms.reshape(devices, -1)], axis=1)
    back = lax.all_to_all(payload, "gx", split_axis=0, concat_axis=0, tiled=True)
    split = CAP * outc * 128
    returned = back[:, :split].reshape(slots, outc * 128)
    answer = jnp.dot(pick, returned, preferred_element_type=F32).astype(BF).reshape(held, outc, 128)
    stencil_grad = jnp.sum(back[:, split:].astype(F32), axis=0).reshape(-1, 27 * channels)
    return answer, stencil_grad


def solution(mesh):
    points = P(("grp", "gx"), None, None)
    flat = P(("grp", "gx"), None)
    return jax.shard_map(
        shards,
        mesh=mesh,
        in_specs=(points, points, flat, flat, flat, points) + (P(),) * 10,
        out_specs=(points, flat),
        check_vma=False,
    )
```

time: 875 us -> 205 us (0.23); the launches traced: 865 us -> 206 us
  other arithmetic: 431 us -> 6.65 us
  local copies, waits for them, and re-layouts: 225 us -> 23.1 us
  waiting for transfers between devices: 107 us -> 0.01 us
  Pallas kernels: 0 us -> 83 us
  blocking collectives: 0 us -> 79.7 us
  matrix products: 43.7 us -> 0.5 us
  starting transfers between devices: 41.8 us -> 11.7 us
  between operations: 16 us -> 0.84 us
    scatter-add x10 -> x0, other arithmetic: 425 us -> none  [the longest x8 422 us: spread(): grid_sum.at[:, cell_ids.reshape(-1)]]
    gather x9 -> x0, local copies, waits for them, and re-layouts: 131 us -> none  [the longest x8 130 us: query_points(): jnp.take(latent_flat, cell_ids.reshape(-1), axis=1)]
    pallas_call x0 -> x3, Pallas kernels: none -> 83 us  [the longest x2 58.1 us: scatter_points(): pl.pallas_call(functools.partial(scatter_kernel, keep), out_shape=shapes,...]
    all_to_all x0 -> x1, blocking collectives: none -> 79.7 us  [shards(): lax.all_to_all(payload, 'gx', split_axis=0, concat_axis=0, tiled=True)]
    unnamed x2 -> x0, waiting for transfers between devices: 74.7 us -> none
    dot_general x74 -> x2, matrix products: 43.7 us -> 0.5 us  [the longest x1 0.31 us: shards(): sent = jnp.dot(pick.T, packed, preferred_element_type=F32).astype(BF)]
    all_to_all x6 -> x1, waiting for transfers between devices: 30.2 us -> 0.01 us  [shards(): pts = lax.all_to_all(sent, 'gx', split_axis=0, concat_axis=0, tiled=True)]
    reshape x9 -> x7, local copies, waits for them, and re-layouts: 31.4 us -> 4.99 us  [the longest x1 1.4 us: shards(): stencil_weight.reshape(9, 3, channels, channels).transpose(0, 2, 1, 3)]
  transfers between devices with their start and end apart: 12 -> 3, of which waited for: 8 -> 0; matrix products, arithmetic and copies ran while one was open for 3% -> 6% of each run, Pallas kernels for 0% -> 14%
where the time goes in v1:
time: 205 us; the launch traced here: 206 us
  Pallas kernels  83 us (40%)
  blocking collectives  79.7 us (39%)
  local copies, waits for them, and re-layouts  23.1 us (11%)
  starting transfers between devices  11.7 us (6%)
  other arithmetic  6.65 us (3%)
    all_to_all x1, blocking collectives, shards(): lax.all_to_all(payload, 'gx', split_axis=0, concat_axis=0, tiled=True)  79.7 us
    pallas_call x2, Pallas kernels, scatter_points(): pl.pallas_call(functools.partial(scatter_kernel, keep), out_shape=shapes,...  58.1 us
    pallas_call x1, Pallas kernels, level(): pl.pallas_call(level_kernel, out_shape=[jax.ShapeDtypeStruct((slots, out_...  24.9 us
    all_to_all x1, starting transfers between devices, shards(): pts = lax.all_to_all(sent, 'gx', split_axis=0, concat_axis=0, tiled=True)  7.38 us
    unnamed x14, local copies, waits for them, and re-layouts  6.34 us
  transfers between devices with their start and end apart: 3, of which 0 were waited for; matrix products, arithmetic and copies ran while one was open for 6% of the time, Pallas kernels for 14%

profile of v1, /device:TPU:0, one launch (start us, length us, event | category | flops | bytes accessed | tf_op | source)
XLA Modules:
  0.0 205.6 jit_solution(17724132182262247656)
XLA Ops:
  0.6 0.9 convert_reduce_fusion.3
  2.2 0.7 convert_bitcast_fusion
  2.9 0.7 fusion.11
  3.7 0.7 copy.67
  4.4 1.6 concatenate.6
  6.3 0.7 all_to_all.14
  7.1 7.4 %all-to-all-start = ((bf16[16,2,3072]{2,1,0:T(2,128)(2,1)}), bf16[16,2,3072]{2,1,0:T(2,128)(2,1)S(1)}, u32[]{:S(2)}, u32[]{:S(2)}) async-start(bf16[16,2,3072]{2,1,0:T(2,128)(2,1)} %all_to_all.14), calls=%async_computation | async-start | bytes 393216 | tf_op jit(solution)/shard_map/all_to_all | solution.py:285
  14.5 1.3 pad.14.out_w_ref
  15.7 0.8 copy.74
  16.5 0.8 copy.71
  17.9 0.7 pad.13.value_w_ref
  18.6 1.4 copy.72.inner_ref
  20.0 1.3 copy.73.bias_ref
  21.3 1.3 copy.78.bias_ref
  22.7 1.4 copy.75.inner_ref
  24.0 1.4 copy.76.bias_ref
  25.4 1.4 copy.88
  26.8 1.1 reshape.72.weight_ref
  28.6 0.7 convert_reduce_fusion.4
  30.1 0.7 select_reduce_fusion.order_ref
  30.8 28.5 %shard_map.167.own_ref = bf16[64,6144]{1,0:T(8,128)(2,1)} custom-call(s32[32]{0:T(128)} %select_reduce_fusion.order_ref, s32[1]{0:T(128)} %bitcast.6.count_ref, f32[32,24,128]{2,1,0:T(8,128)} %copy-done, bf16[64,24]{1,0:T(8,128)(2,1)} %pad.12.value_w_ref, f32[64,3]{1,0:T(8,128)} %copy.72.inner_ref, f32[64,1]{1,0:T(8,128)} %copy.73.bias_ref, ...), custom_call_target="tpu_custom_call" | custom-call | flops 8589934592 | bytes 4194304 | tf_op jit(solution)/shard_map/pallas_call | solution.py:107
  59.2 1.3 fusion.14
  60.5 1.3 collective-permute-start.1
  61.8 3.1 %collective-permute-start = (bf16[64,4096]{1,0:T(8,128)(2,1)S(1)}, bf16[64,4096]{1,0:T(8,128)(2,1)S(1)}, u32[]{:S(2)}, u32[]{:S(2)}) collective-permute-start(bf16[64,4096]{1,0:T(8,128)(2,1)S(1)} %get-tuple-element.11), channel_id=1, source_target_pairs={{0,1},{1,2},{2,3},{3,4},{4,5},{5,6},{6,7},{7,8},{8,9},{9,10},{10,1... | collective-permute-start | bytes 1572872 | tf_op jit(solution)/shard_map/ppermute | solution.py:307
  64.9 29.6 %shard_map.168 = (f32[64,6144]{1,0:T(8,128)}, bf16[8,512,512]{2,1,0:T(8,128)(2,1)}) custom-call(s32[32]{0:T(128)} %select_reduce_fusion.order_ref, s32[1]{0:T(128)} %bitcast.6.count_ref, f32[32,24,128]{2,1,0:T(8,128)} %copy-done, bf16[64,24]{1,0:T(8,128)(2,1)} %pad.13.value_w_ref, f32[64,3]{1,0:T(8,128)} %copy.75.inner_ref, f32[64,1]{1,0:T(8,128)} %copy.76.bias_ref, ...), custom_call_target="tpu_custom_call" | custom-call | flops 8589934592 | bytes 4194304 | tf_op jit(solution)/shard_map/pallas_call | solution.py:107
  94.5 0.8 copy-done.1
  95.5 24.9 %shard_map.169 = (f32[32,8,128]{2,1,0:T(8,128)}, bf16[64,1728]{1,0:T(8,128)(2,1)}) custom-call(s32[32]{0:T(128)} %select_reduce_fusion.order_ref, s32[1]{0:T(128)} %bitcast.6.count_ref, s32[1]{0:T(128)} %bitcast.7.edge_ref, f32[32,24,128]{2,1,0:T(8,128)} %copy-done, bf16[64,6144]{1,0:T(8,128)(2,1)} %shard_map.167.own_ref, bf16[64,4096]{1,0:T(8,128)(2,1)} %copy-done.2, ...), custom_call_target="tpu_custom_call" | custom-call | tf_op jit(solution)/shard_map/pallas_call | solution.py:231
  120.5 0.9 slice.34
  121.4 1.2 reshape.74
  123.1 0.8 reduce.2
  124.0 79.7 %all_to_all.21 = bf16[16,2,3968]{2,1,0:T(2,128)(2,1)S(1)} all-to-all(bf16[16,2,3968]{2,1,0:T(2,128)(2,1)S(1)} %reshape.82), channel_id=1, replica_groups=mesh['grp'=2,'gx'=16] {'gx'}, dimensions={0} | all-to-all | bytes 507904 | tf_op jit(solution)/shard_map/all_to_all | solution.py:324
  204.9 0.7 reshape.77
  (33 shorter events, 5.2 us)
Async XLA Ops:
  7.1 20.8 %all-to-all-start = ((bf16[16,2,3072]{2,1,0:T(2,128)(2,1)}), bf16[16,2,3072]{2,1,0:T(2,128)(2,1)S(1)}, u32[]{:S(2)}, u32[]{:S(2)}) async-start(bf16[16,2,3072]{2,1,0:T(2,128)(2,1)} %all_to_all.14), calls=%async_computation | async-start | bytes 393216 | tf_op jit(solution)/shard_map/all_to_all | solution.py:285
  28.0 2.8 %copy-start = (f32[32,24,128]{2,1,0:T(8,128)}, f32[32,24,128]{2,1,0:T(8,128)S(1)}, u32[]{:S(2)}) copy-start(f32[32,24,128]{2,1,0:T(8,128)S(1)} %reshape.78.pts_ref) | copy-start | bytes 1179652
  60.5 34.0 %collective-permute-start.1 = (bf16[64,4096]{1,0:T(8,128)(2,1)S(1)}, bf16[64,4096]{1,0:T(8,128)(2,1)S(1)}, u32[]{:S(2)}, u32[]{:S(2)}) collective-permute-start(bf16[64,4096]{1,0:T(8,128)(2,1)S(1)} %get-tuple-element.10), channel_id=1, source_target_pairs={{1,0},{2,1},{3,2},{4,3},{5,4},{6,5},{7,6},{8,7},{9,8},{10,9},{11,1... | collective-permute-start | bytes 1572872 | tf_op jit(solution)/shard_map/ppermute | solution.py:308
  61.8 32.7 %collective-permute-start = (bf16[64,4096]{1,0:T(8,128)(2,1)S(1)}, bf16[64,4096]{1,0:T(8,128)(2,1)S(1)}, u32[]{:S(2)}, u32[]{:S(2)}) collective-permute-start(bf16[64,4096]{1,0:T(8,128)(2,1)S(1)} %get-tuple-element.11), channel_id=1, source_target_pairs={{0,1},{1,2},{2,3},{3,4},{4,5},{5,6},{6,7},{7,8},{8,9},{9,10},{10,1... | collective-permute-start | bytes 1572872 | tf_op jit(solution)/shard_map/ppermute | solution.py:307
  94.5 0.8 copy-start.1
  94.5 1.0 copy-start.2

commit v2 on v1

v2 whole, which is shorter than its diff:
```python
import jax
import jax.numpy as jnp
from jax import lax
from jax.experimental import pallas as pl
from jax.experimental.pallas import tpu as pltpu
from jax.sharding import PartitionSpec as P

CAP = 2
GXD = 2
GY = 16
GZ = 128
PLANE = GY * GZ
BASE = GXD * PLANE
EXT = (GXD + 1) * PLANE
PADDED = (GY + 2) * GZ
UNROLL = 16
BF = jnp.bfloat16
F32 = jnp.float32
NT = (((1,), (1,)), ((), ()))
VMEM_LIMIT = 60 * 1024 * 1024


def smooth(v):
    return 0.5 * v * (1.0 + jnp.tanh(v * (0.7978845608 + (0.7978845608 * 0.044715) * (v * v))))


def smooth_slope(v):
    square = v * v
    t = jnp.tanh(v * (0.7978845608 + (0.7978845608 * 0.044715) * square))
    inner = 0.7978845608 + (3.0 * 0.7978845608 * 0.044715) * square
    return 0.5 * (1.0 + t) + 0.5 * v * (1.0 - t * t) * inner


def scatter_kernel(
    order_ref, count_ref, cells_ref, pts_ref, lift_ref, query_ref, *rest
):
    nets, (own_ref, grad_ref, kept_ref, acc0_ref, acc1_ref, part_ref) = rest[:6], rest[6:]
    channels = lift_ref.shape[1]
    pair = 2 * channels
    acc0_ref[...] = jnp.zeros_like(acc0_ref)
    acc1_ref[...] = jnp.zeros_like(acc1_ref)
    upper = lax.broadcasted_iota(jnp.int32, (1, pair), 1) >= channels
    corner_z = jnp.where(upper, 1.0, 0.0)
    lane_bit = lax.broadcasted_iota(jnp.int32, (128, pair), 1) // channels

    def twice(values):
        return jnp.concatenate([values, values], axis=1)

    lift = jnp.concatenate([twice(lift_ref[...]), jnp.zeros((16, pair), F32)], axis=0).astype(BF)
    query = jnp.concatenate(
        [jnp.zeros((8, pair), F32), twice(query_ref[...]), jnp.zeros((8, pair), F32)], axis=0
    ).astype(BF)
    layers = []
    for k in range(2):
        inner_ref, bias_ref, outer_ref = nets[3 * k : 3 * k + 3]
        outer = outer_ref[...].astype(F32)
        blank = jnp.zeros_like(outer)
        both = jnp.concatenate(
            [jnp.concatenate([outer, blank], axis=1), jnp.concatenate([blank, outer], axis=1)], axis=0
        ).astype(BF)
        inner = [twice(inner_ref[i : i + 1, :]) for i in range(3)]
        layers.append((inner, twice(bias_ref[...]) + corner_z * inner[2], both))

    @pl.loop(0, count_ref[0])
    def _(index):
        slot = order_ref[index]
        points = jnp.transpose(pts_ref[slot], (1, 0))
        rounded = points.astype(BF)
        values = [
            jnp.dot(rounded, weight, preferred_element_type=F32).astype(BF).astype(F32)
            for weight in (lift, query)
        ]
        fraction = [jnp.broadcast_to(points[:, 12 + i : 13 + i], (128, pair)) for i in range(3)]
        bits = jnp.broadcast_to(points[:, 18:19], (128, pair)).astype(jnp.int32) >> lane_bit
        live = [((bits >> (2 * t)) & 1).astype(F32) for t in range(4)]
        for k in range(2):
            inner, start, both = layers[k]
            base = start - (fraction[0] * inner[0] + fraction[1] * inner[1] + fraction[2] * inner[2])
            for t in range(4):
                hidden = smooth(base + ((t // 2) * inner[0] + (t % 2) * inner[1])).astype(BF)
                out = lax.dot_general(hidden, both, NT, preferred_element_type=F32)
                out = (out * live[t]).astype(BF)
                if k == 1:
                    kept_ref[index, t] = out
                part_ref[:, 4 * k + t, :] = out.astype(F32) * values[k]

        @pl.loop(0, 128 // UNROLL)
        def _(group):
            for u in range(0, UNROLL, 2):
                place = group * UNROLL + u
                even, odd = cells_ref[slot, place], cells_ref[slot, place + 1]
                acc0_ref[even] += part_ref[place]
                acc1_ref[odd] += part_ref[place + 1]

    for row in range((GXD + 1) * GY):
        for k, out_ref in ((0, own_ref), (1, grad_ref)):
            total = None
            for t in range(4):
                source = row - (t // 2) * GY - t % 2
                if 0 <= source < GXD * GY:
                    for acc_ref in (acc0_ref, acc1_ref):
                        piece = acc_ref[source * GZ : (source + 1) * GZ, 4 * k + t, :]
                        total = piece if total is None else total + piece
            flat = jnp.transpose(total, (1, 0))
            flat = flat[0:channels] + pltpu.roll(flat[channels:], 1, 1)
            out_ref[:, row * GZ : (row + 1) * GZ] = flat.astype(out_ref.dtype)


def scatter_points(order, count, cells, pts, lift, query, *nets):
    channels = lift.shape[1]
    slots = pts.shape[0]
    smem = pl.BlockSpec(memory_space=pltpu.SMEM)
    vmem = pl.BlockSpec(memory_space=pltpu.VMEM)
    return pl.pallas_call(
        scatter_kernel,
        out_shape=[
            jax.ShapeDtypeStruct((channels, EXT), BF),
            jax.ShapeDtypeStruct((channels, EXT), F32),
            jax.ShapeDtypeStruct((slots, 4, 128, 2 * channels), BF),
        ],
        in_specs=[smem] * 3 + [vmem] * 9,
        out_specs=[vmem] * 3,
        scratch_shapes=[
            pltpu.VMEM((BASE, 8, 2 * channels), F32),
            pltpu.VMEM((BASE, 8, 2 * channels), F32),
            pltpu.VMEM((128, 8, 2 * channels), F32),
        ],
        compiler_params=pltpu.CompilerParams(vmem_limit_bytes=VMEM_LIMIT),
    )(order, count, cells, pts, lift, query, *nets)


def level_kernel(
    order_ref, count_ref, edge_ref, cells_ref, own_ref, left_ref, right_ref, grad_ref, kept_ref,
    weight_ref, bias_ref, out_w_ref, pred_ref, sg_ref, lz_ref, pre_ref, lat_ref, table_ref, got_ref,
    gp_ref, win_ref, sum_ref,
):
    channels = own_ref.shape[0]
    inside = jnp.where(edge_ref[0] > 0, 0.0, 1.0).astype(F32)
    z = lax.broadcasted_iota(jnp.int32, (channels, PLANE), 1) % GZ
    first, last = z == 0, z == GZ - 1
    lz_ref[...] = jnp.zeros_like(lz_ref)

    def put_plane(index, plane):
        start = index * PADDED + GZ
        lz_ref[channels : 2 * channels, start : start + PLANE] = plane.astype(BF)
        below = jnp.where(first, 0.0, pltpu.roll(plane, 1, 1))
        above = jnp.where(last, 0.0, pltpu.roll(plane, PLANE - 1, 1))
        lz_ref[0:channels, start : start + PLANE] = below.astype(BF)
        lz_ref[2 * channels :, start : start + PLANE] = above.astype(BF)

    def own(k):
        return own_ref[:, k * PLANE : (k + 1) * PLANE].astype(F32)

    put_plane(0, left_ref[:, 0:PLANE].astype(F32))
    put_plane(1, own(0) + left_ref[:, PLANE:].astype(F32))
    put_plane(2, own(1))
    put_plane(3, (own(2) + right_ref[:, 0:PLANE].astype(F32)) * inside)
    put_plane(4, right_ref[:, PLANE:].astype(F32))

    for x in range(3):
        total = None
        for a in range(3):
            start = (x + a) * PADDED
            terms = jnp.dot(
                weight_ref[a * 3 * channels : (a + 1) * 3 * channels, :],
                lz_ref[:, start : start + PADDED],
                preferred_element_type=F32,
            )
            for e in range(3):
                piece = terms[e * channels : (e + 1) * channels, e * GZ : e * GZ + PLANE]
                total = piece if total is None else total + piece
        pre = total + bias_ref[...]
        pre_ref[x] = pre
        out = smooth(pre)
        if x == 2:
            out = out * inside
        out = out.astype(BF).astype(F32)
        lat_ref[0:channels, x * PLANE : (x + 1) * PLANE] = out
        lat_ref[channels:, x * PLANE : (x + 1) * PLANE] = pltpu.roll(out, PLANE - 1, 1)
    for row in range((GXD + 1) * GY):
        flat = jnp.transpose(lat_ref[:, row * GZ : (row + 1) * GZ], (1, 0))
        for t in range(4):
            target = row - (t // 2) * GY - t % 2
            if 0 <= target < GXD * GY:
                table_ref[target * GZ : (target + 1) * GZ, t, :] = flat

    pred_ref[...] = jnp.zeros_like(pred_ref)
    out_w = jnp.concatenate([out_w_ref[...], out_w_ref[...]], axis=1).astype(BF)

    @pl.loop(0, count_ref[0])
    def _(index):
        slot = order_ref[index]

        @pl.loop(0, 128 // UNROLL)
        def _(group):
            for u in range(UNROLL):
                place = group * UNROLL + u
                got_ref[place] = table_ref[cells_ref[slot, place]]

        queried = None
        for t in range(4):
            term = got_ref[:, t, :] * kept_ref[index, t].astype(F32)
            queried = term if queried is None else queried + term
        pred_ref[slot] = lax.dot_general(out_w, queried.astype(BF), NT, preferred_element_type=F32)

    for x in range(3):
        grad = grad_ref[:, x * PLANE : (x + 1) * PLANE] * smooth_slope(pre_ref[x])
        if x == 2:
            grad = grad * inside
        gp_ref[0:channels, :] = jnp.where(last, 0.0, pltpu.roll(grad, PLANE - 1, 1)).astype(BF)
        gp_ref[channels : 2 * channels, :] = grad.astype(BF)
        gp_ref[2 * channels :, :] = jnp.where(first, 0.0, pltpu.roll(grad, 1, 1)).astype(BF)
        for k in range(9):
            start = (x + k // 3) * PADDED + (k % 3) * GZ
            win_ref[k * channels : (k + 1) * channels, :] = lz_ref[
                channels : 2 * channels, start : start + PLANE
            ]
        term = lax.dot_general(gp_ref[...], win_ref[...], NT, preferred_element_type=F32)
        if x == 0:
            sum_ref[...] = term
        else:
            sum_ref[...] += term
    for k in range(27):
        f, place = k % 3, k // 3
        sg_ref[:, k * channels : (k + 1) * channels] = sum_ref[
            f * channels : (f + 1) * channels, place * channels : (place + 1) * channels
        ].astype(BF)


def level(order, count, edge, cells, own, left, right, grad, kept, weight, bias, out_w):
    channels = own.shape[0]
    slots = cells.shape[0]
    smem = pl.BlockSpec(memory_space=pltpu.SMEM)
    vmem = pl.BlockSpec(memory_space=pltpu.VMEM)
    return pl.pallas_call(
        level_kernel,
        out_shape=[
            jax.ShapeDtypeStruct((slots, out_w.shape[0], 128), F32),
            jax.ShapeDtypeStruct((channels, 27 * channels), BF),
        ],
        in_specs=[smem] * 4 + [vmem] * 8,
        out_specs=[vmem] * 2,
        scratch_shapes=[
            pltpu.VMEM((3 * channels, 5 * PADDED), BF),
            pltpu.VMEM((3, channels, PLANE), F32),
            pltpu.VMEM((2 * channels, EXT), F32),
            pltpu.VMEM((BASE, 4, 2 * channels), F32),
            pltpu.VMEM((128, 4, 2 * channels), F32),
            pltpu.VMEM((3 * channels, PLANE), BF),
            pltpu.VMEM((9 * channels, PLANE), BF),
            pltpu.VMEM((3 * channels, 9 * channels), F32),
        ],
        compiler_params=pltpu.CompilerParams(vmem_limit_bytes=VMEM_LIMIT),
    )(order, count, edge, cells, own, left, right, grad, kept, weight, bias, out_w)


def shards(
    point_fraction, point_features, base_cell, corner_bits, owner_map, cotangent, lift_weight,
    encode_inner, encode_bias, encode_outer, stencil_weight, stencil_bias, decode_inner,
    decode_bias, decode_outer, output_weight,
):
    devices = lax.axis_size("gx")
    me = lax.axis_index("gx")
    slots = devices * CAP
    channels = lift_weight.shape[0]
    target = owner_map[:, 0]
    held = target.shape[0]
    matching = target[:, None] == target[None, :]
    earlier = jnp.arange(held)[None, :] < jnp.arange(held)[:, None]
    ranking = jnp.sum(jnp.logical_and(matching, earlier), axis=1)
    places = target * CAP + ranking
    pick = (places[:, None] == jnp.arange(slots)[None, :]).astype(BF)

    packed = jnp.concatenate(
        [
            point_features,
            cotangent,
            point_fraction,
            jnp.zeros((held, 1, 128), BF),
            (base_cell // GZ).astype(BF)[:, None],
            (base_cell % GZ).astype(BF)[:, None],
            corner_bits.astype(BF)[:, None],
            jnp.ones((held, 1, 128), BF),
            jnp.zeros((held, 4, 128), BF),
        ],
        axis=1,
    ).reshape(held, -1)
    sent = jnp.dot(pick.T, packed, preferred_element_type=F32).astype(BF)
    pts = lax.all_to_all(sent, "gx", split_axis=0, concat_axis=0, tiled=True)
    pts = pts.reshape(slots, 24, 128).astype(F32)

    active = pts[:, 19, 0] > 0.5
    before = jnp.arange(slots)[None, :] < jnp.arange(slots)[:, None]
    count = jnp.sum(active.astype(jnp.int32))
    ahead_on = jnp.sum((before & active[None, :]).astype(jnp.int32), axis=1)
    ahead_off = jnp.sum((before & ~active[None, :]).astype(jnp.int32), axis=1)
    place = jnp.where(active, ahead_on, count + ahead_off)
    order = jnp.sum(
        jnp.where(place[None, :] == jnp.arange(slots)[:, None], jnp.arange(slots)[None, :], 0), axis=1
    ).astype(jnp.int32)
    count = count.reshape(1)
    edge = (me == devices - 1).astype(jnp.int32).reshape(1)

    cells = (pts[:, 16] * GZ + pts[:, 17]).astype(jnp.int32)
    query = jnp.pad(output_weight.astype(F32), ((0, 4), (0, 0)))
    own, grad, kept = scatter_points(
        order, count, cells, pts, lift_weight.astype(F32).T, query,
        encode_inner.T, encode_bias[None], encode_outer, decode_inner.T, decode_bias[None], decode_outer,
    )
    up = [(i, i + 1) for i in range(devices - 1)]
    down = [(i + 1, i) for i in range(devices - 1)]
    left = lax.ppermute(own[:, PLANE:], "gx", up)
    right = lax.ppermute(own[:, :BASE], "gx", down)
    weight = (
        stencil_weight.reshape(9, 3, channels, channels)
        .transpose(0, 2, 1, 3)
        .reshape(9 * channels, 3 * channels)
    )
    predicted, terms = level(
        order, count, edge, cells, own, left, right, grad, kept, weight, stencil_bias[:, None], query
    )
    outc = output_weight.shape[0]
    predicted = predicted[:, :outc].astype(BF).reshape(devices, -1)
    payload = jnp.concatenate([predicted, terms.reshape(devices, -1)], axis=1)
    back = lax.all_to_all(payload, "gx", split_axis=0, concat_axis=0, tiled=True)
    split = CAP * outc * 128
    returned = back[:, :split].reshape(slots, outc * 128)
    answer = jnp.dot(pick, returned, preferred_element_type=F32).astype(BF).reshape(held, outc, 128)
    stencil_grad = jnp.sum(back[:, split:].astype(F32), axis=0).reshape(-1, 27 * channels)
    return answer, stencil_grad


def solution(mesh):
    points = P(("grp", "gx"), None, None)
    flat = P(("grp", "gx"), None)
    return jax.shard_map(
        shards,
        mesh=mesh,
        in_specs=(points, points, flat, flat, flat, points) + (P(),) * 10,
        out_specs=(points, flat),
        check_vma=False,
    )
```

time: 205 us -> 151 us (0.74)
  blocking collectives: 79.7 us -> 51.1 us
  Pallas kernels: 83 us -> 58.6 us
  local copies, waits for them, and re-layouts: 23.1 us -> 12 us
  waiting for transfers between devices: 0.01 us -> 6.45 us
  other arithmetic: 6.65 us -> 9.75 us
    all_to_all x1, blocking collectives: 79.7 us -> 51.1 us  [shards(): lax.all_to_all(payload, 'gx', split_axis=0, concat_axis=0, tiled=True)]
    pallas_call x2 -> x1, Pallas kernels: 58.1 us -> 35 us  [scatter_points(): pl.pallas_call(scatter_kernel, out_shape=[jax.ShapeDtypeStruct((channels,...]
    all_to_all x1, waiting for transfers between devices: 0.01 us -> 6.45 us  [shards(): pts = lax.all_to_all(sent, 'gx', split_axis=0, concat_axis=0, tiled=True)]
    unnamed x14, local copies, waits for them, and re-layouts: 6.34 us -> 2.05 us
    broadcast_in_dim x2 -> x0, local copies, waits for them, and re-layouts: 2.7 us -> none  [the longest x1 1.36 us: shards(): decode_bias[:, None]]
    pad x3 -> x0, local copies, waits for them, and re-layouts: 2.56 us -> none  [the longest x1 1.26 us: shards(): out_w = jnp.pad(output_weight, ((0, 4), (0, 0)))]
  transfers between devices with their start and end apart: 3 -> 3, of which waited for: 0 -> 1; matrix products, arithmetic and copies ran while one was open for 6% -> 3% of each run, Pallas kernels for 14% -> 0%
where the time goes in v2:
time: 151 us
  Pallas kernels  58.6 us (39%)
  blocking collectives  51.1 us (34%)
  local copies, waits for them, and re-layouts  12 us (8%)
  starting transfers between devices  11.7 us (8%)
  other arithmetic  9.75 us (6%)
  waiting for transfers between devices  6.45 us (4%)
    all_to_all x1, blocking collectives, shards(): lax.all_to_all(payload, 'gx', split_axis=0, concat_axis=0, tiled=True)  51.1 us
    pallas_call x1, Pallas kernels, scatter_points(): pl.pallas_call(scatter_kernel, out_shape=[jax.ShapeDtypeStruct((channels,...  35 us
    pallas_call x1, Pallas kernels, level(): pl.pallas_call(level_kernel, out_shape=[jax.ShapeDtypeStruct((slots, out_...  23.6 us
    all_to_all x1, starting transfers between devices, shards(): pts = lax.all_to_all(sent, 'gx', split_axis=0, concat_axis=0, tiled=True)  7.39 us
    all_to_all x1, waiting for transfers between devices, shards(): pts = lax.all_to_all(sent, 'gx', split_axis=0, concat_axis=0, tiled=True)  6.45 us
    ppermute x1, starting transfers between devices, shards(): left = lax.ppermute(own[:, PLANE:], 'gx', up)  3.06 us
  transfers between devices with their start and end apart: 3, of which 1 were waited for; matrix products, arithmetic and copies ran while one was open for 3% of the time, Pallas kernels for 0%

profile of v2, /device:TPU:0, one launch (start us, length us, event | category | flops | bytes accessed | tf_op | source)
XLA Modules:
  0.0 151.0 jit_solution(12542255372360711845)
XLA Ops:
  0.6 0.9 convert_reduce_fusion.3
  1.6 0.7 fusion.13
  2.2 0.7 convert_bitcast_fusion.2
  2.9 0.7 fusion.11
  3.7 0.7 copy.50
  4.4 1.6 %concatenate.6 = bf16[16,24,128]{2,1,0:T(8,128)(2,1)S(1)} concatenate(bf16[16,8,128]{2,1,0:T(8,128)(2,1)} %param.17, bf16[16,4,128]{2,1,0:T(4,128)(2,1)} %param.21, bf16[16,3,128]{2,1,0:T(4,128)(2,1)S(1)} %copy.50, bf16[16,1,128]{2,1,0:T(2,128)(2,1)S(1)} %broadcast_in_dim.48, bf16[16,1,128]{2,1,0:T(2,128)(2,1)S(1)} %copy.51, bf16[16,1,128]{2,1,0:T(2,128)(2,1)S(1)} %copy.52, ...), dimensions={1} | concatenate | bytes 196608 | tf_op jit(solution)/shard_map/concatenate | solution.py:274
  6.4 0.8 all_to_all.14
  7.1 7.4 %all-to-all-start = ((bf16[16,2,3072]{2,1,0:T(2,128)(2,1)}), bf16[16,2,3072]{2,1,0:T(2,128)(2,1)S(1)}, u32[]{:S(2)}, u32[]{:S(2)}) async-start(bf16[16,2,3072]{2,1,0:T(2,128)(2,1)} %all_to_all.14), calls=%async_computation | async-start | bytes 393216 | tf_op jit(solution)/shard_map/all_to_all | solution.py:289
  14.5 1.3 pad_convert_fusion.query_ref.out_w_ref
  15.8 1.3 convert_bitcast_fusion.1.lift_ref
  17.1 6.4 %all-to-all-done = bf16[16,2,3072]{2,1,0:T(2,128)(2,1)S(1)} async-done(((bf16[16,2,3072]{2,1,0:T(2,128)(2,1)}), bf16[16,2,3072]{2,1,0:T(2,128)(2,1)S(1)}, u32[]{:S(2)}, u32[]{:S(2)}) %all-to-all-start) | async-done | bytes 196640 | tf_op jit(solution)/shard_map/all_to_all | solution.py:289
  23.6 0.7 compare_reduce_fusion
  24.3 0.7 convert_reduce_fusion.4
  25.1 0.6 add_select_fusion.2
  25.7 0.6 select_reduce_fusion.order_ref
  26.4 0.6 convert_bitcast_fusion.cells_ref
  27.0 35.0 %shard_map.167 = (bf16[64,6144]{1,0:T(8,128)(2,1)}, f32[64,6144]{1,0:T(8,128)}, bf16[32,4,128,128]{3,2,1,0:T(8,128)(2,1)}) custom-call(s32[32]{0:T(128)} %select_reduce_fusion.order_ref, s32[1]{0:T(128)} %bitcast.6.count_ref, s32[32,128]{1,0:T(8,128)} %convert_bitcast_fusion.cells_ref, f32[32,24,128]{2,1,0:T(8,128)} %copy-done, ...), custom_call_target="tpu_custom_call" | custom-call | tf_op jit(solution)/shard_map/pallas_call | solution.py:114
  62.0 1.3 fusion.14
  63.2 1.3 collective-permute-start.1
  64.5 3.1 %collective-permute-start = (bf16[64,4096]{1,0:T(8,128)(2,1)S(1)}, bf16[64,4096]{1,0:T(8,128)(2,1)S(1)}, u32[]{:S(2)}, u32[]{:S(2)}) collective-permute-start(bf16[64,4096]{1,0:T(8,128)(2,1)S(1)} %get-tuple-element.13), channel_id=1, source_target_pairs={{0,1},{1,2},{2,3},{3,4},{4,5},{5,6},{6,7},{7,8},{8,9},{9,10},{10,1... | collective-permute-start | bytes 1572872 | tf_op jit(solution)/shard_map/ppermute | solution.py:312
  67.6 0.7 copy.57.bias_ref
  68.3 0.4 copy.69
  68.7 1.1 reshape.76.weight_ref
  69.8 0.8 copy-done.1
  70.8 23.6 %shard_map.168 = (f32[32,8,128]{2,1,0:T(8,128)}, bf16[64,1728]{1,0:T(8,128)(2,1)}) custom-call(s32[32]{0:T(128)} %select_reduce_fusion.order_ref, s32[1]{0:T(128)} %bitcast.6.count_ref, s32[1]{0:T(128)} %bitcast.7.edge_ref, s32[32,128]{1,0:T(8,128)} %convert_bitcast_fusion.cells_ref, bf16[64,6144]{1,0:T(8,128)(2,1)} %get-tuple-element.7.own_ref, ...), custom_call_target="tpu_custom_call" | custom-call | tf_op jit(solution)/shard_map/pallas_call | solution.py:235
  94.4 0.9 slice.42
  95.4 1.2 reshape.78
  96.6 0.5 broadcast.45
  97.1 0.8 reduce.2
  98.0 51.1 %all_to_all.21 = bf16[16,2,3968]{2,1,0:T(2,128)(2,1)S(1)} all-to-all(bf16[16,2,3968]{2,1,0:T(2,128)(2,1)S(1)} %reshape.86), channel_id=1, replica_groups=mesh['grp'=2,'gx'=16] {'gx'}, dimensions={0} | all-to-all | bytes 507904 | tf_op jit(solution)/shard_map/all_to_all | solution.py:325
  149.6 0.6 reshape.80
  150.3 0.7 reshape.81
  (31 shorter events, 1.5 us)
Async XLA Ops:
  0.6 67.0 %copy-start.4 = (f32[64]{0:T(128)S(1)}, f32[64]{0:T(128)}, u32[]{:S(2)}) copy-start(f32[64]{0:T(128)} %param.27) | copy-start | bytes 772
  0.6 67.7 %copy-start.3 = (bf16[27,64,64]{2,1,0:T(8,128)(2,1)S(1)}, bf16[27,64,64]{2,1,0:T(8,128)(2,1)}, u32[]{:S(2)}) copy-start(bf16[27,64,64]{2,1,0:T(8,128)(2,1)} %param.26) | copy-start | bytes 663556
  7.1 16.4 %all-to-all-start = ((bf16[16,2,3072]{2,1,0:T(2,128)(2,1)}), bf16[16,2,3072]{2,1,0:T(2,128)(2,1)S(1)}, u32[]{:S(2)}, u32[]{:S(2)}) async-start(bf16[16,2,3072]{2,1,0:T(2,128)(2,1)} %all_to_all.14), calls=%async_computation | async-start | bytes 393216 | tf_op jit(solution)/shard_map/all_to_all | solution.py:289
  23.6 3.4 %copy-start = (f32[32,24,128]{2,1,0:T(8,128)}, f32[32,24,128]{2,1,0:T(8,128)S(1)}, u32[]{:S(2)}) copy-start(f32[32,24,128]{2,1,0:T(8,128)S(1)} %reshape.82.pts_ref) | copy-start | bytes 1179652
  63.2 6.5 %collective-permute-start.1 = (bf16[64,4096]{1,0:T(8,128)(2,1)S(1)}, bf16[64,4096]{1,0:T(8,128)(2,1)S(1)}, u32[]{:S(2)}, u32[]{:S(2)}) collective-permute-start(bf16[64,4096]{1,0:T(8,128)(2,1)S(1)} %get-tuple-element.12), channel_id=1, source_target_pairs={{1,0},{2,1},{3,2},{4,3},{5,4},{6,5},{7,6},{8,7},{9,8},{10,9},{11,1... | collective-permute-start | bytes 1572872 | tf_op jit(solution)/shard_map/ppermute | solution.py:313
  64.5 5.2 %collective-permute-start = (bf16[64,4096]{1,0:T(8,128)(2,1)S(1)}, bf16[64,4096]{1,0:T(8,128)(2,1)S(1)}, u32[]{:S(2)}, u32[]{:S(2)}) collective-permute-start(bf16[64,4096]{1,0:T(8,128)(2,1)S(1)} %get-tuple-element.13), channel_id=1, source_target_pairs={{0,1},{1,2},{2,3},{3,4},{4,5},{5,6},{6,7},{7,8},{8,9},{9,10},{10,1... | collective-permute-start | bytes 1572872 | tf_op jit(solution)/shard_map/ppermute | solution.py:312
  69.8 0.8 copy-start.1
  69.8 1.0 copy-start.2

commit v3 on v2

--- a/solution.py
+++ b/solution.py
@@ -1,3 +1,5 @@
+import functools
+
 import jax
 import jax.numpy as jnp
 from jax import lax
@@ -14,6 +16,7 @@
 EXT = (GXD + 1) * PLANE
 PADDED = (GY + 2) * GZ
 UNROLL = 16
+ACCS = 2
 BF = jnp.bfloat16
 F32 = jnp.float32
 NT = (((1,), (1,)), ((), ()))
@@ -32,13 +35,13 @@
 
 
 def scatter_kernel(
-    order_ref, count_ref, cells_ref, pts_ref, lift_ref, query_ref, *rest
+    active_ref, cells_ref, pts_ref, lift_ref, query_ref, *rest
 ):
-    nets, (own_ref, grad_ref, kept_ref, acc0_ref, acc1_ref, part_ref) = rest[:6], rest[6:]
+    nets, (own_ref, grad_ref, kept_ref, part_ref), sums = rest[:6], rest[6:10], rest[10:]
     channels = lift_ref.shape[1]
     pair = 2 * channels
-    acc0_ref[...] = jnp.zeros_like(acc0_ref)
-    acc1_ref[...] = jnp.zeros_like(acc1_ref)
+    for acc_ref in sums:
+        acc_ref[...] = jnp.zeros_like(acc_ref)
     upper = lax.broadcasted_iota(jnp.int32, (1, pair), 1) >= channels
     corner_z = jnp.where(upper, 1.0, 0.0)
     lane_bit = lax.broadcasted_iota(jnp.int32, (128, pair), 1) // channels
@@ -61,9 +64,10 @@
         inner = [twice(inner_ref[i : i + 1, :]) for i in range(3)]
         layers.append((inner, twice(bias_ref[...]) + corner_z * inner[2], both))
 
-    @pl.loop(0, count_ref[0])
-    def _(index):
-        slot = order_ref[index]
+    @pl.loop(0, active_ref.shape[0])
+    def _(slot):
+      @pl.when(active_ref[slot] > 0)
+      def _():
         points = jnp.transpose(pts_ref[slot], (1, 0))
         rounded = points.astype(BF)
         values = [
@@ -81,32 +85,35 @@
                 out = lax.dot_general(hidden, both, NT, preferred_element_type=F32)
                 out = (out * live[t]).astype(BF)
                 if k == 1:
-                    kept_ref[index, t] = out
+                    kept_ref[slot, t] = out
                 part_ref[:, 4 * k + t, :] = out.astype(F32) * values[k]
 
         @pl.loop(0, 128 // UNROLL)
         def _(group):
-            for u in range(0, UNROLL, 2):
+            for u in range(UNROLL):
                 place = group * UNROLL + u
-                even, odd = cells_ref[slot, place], cells_ref[slot, place + 1]
-                acc0_ref[even] += part_ref[place]
-                acc1_ref[odd] += part_ref[place + 1]
-
+                sums[u % ACCS][cells_ref[slot, place]] += part_ref[place]
+
+    eye = jnp.where(
+        lax.broadcasted_iota(jnp.int32, (pair, pair), 0) == lax.broadcasted_iota(jnp.int32, (pair, pair), 1),
+        1.0,
+        0.0,
+    ).astype(BF)
     for row in range((GXD + 1) * GY):
         for k, out_ref in ((0, own_ref), (1, grad_ref)):
             total = None
             for t in range(4):
                 source = row - (t // 2) * GY - t % 2
                 if 0 <= source < GXD * GY:
-                    for acc_ref in (acc0_ref, acc1_ref):
+                    for acc_ref in sums:
                         piece = acc_ref[source * GZ : (source + 1) * GZ, 4 * k + t, :]
                         total = piece if total is None else total + piece
-            flat = jnp.transpose(total, (1, 0))
+            flat = lax.dot_general(eye, total.astype(BF), NT, preferred_element_type=F32)
             flat = flat[0:channels] + pltpu.roll(flat[channels:], 1, 1)
             out_ref[:, row * GZ : (row + 1) * GZ] = flat.astype(out_ref.dtype)
 
 
-def scatter_points(order, count, cells, pts, lift, query, *nets):
+def scatter_points(active, cells, pts, lift, query, *nets):
     channels = lift.shape[1]
     slots = pts.shape[0]
     smem = pl.BlockSpec(memory_space=pltpu.SMEM)
@@ -118,19 +125,18 @@
             jax.ShapeDtypeStruct((channels, EXT), F32),
             jax.ShapeDtypeStruct((slots, 4, 128, 2 * channels), BF),
         ],
-        in_specs=[smem] * 3 + [vmem] * 9,
+        in_specs=[smem] * 2 + [vmem] * 9,
         out_specs=[vmem] * 3,
         scratch_shapes=[
-            pltpu.VMEM((BASE, 8, 2 * channels), F32),
-            pltpu.VMEM((BASE, 8, 2 * channels), F32),
             pltpu.VMEM((128, 8, 2 * channels), F32),
-        ],
+        ]
+        + [pltpu.VMEM((BASE, 8, 2 * channels), F32)] * ACCS,
         compiler_params=pltpu.CompilerParams(vmem_limit_bytes=VMEM_LIMIT),
-    )(order, count, cells, pts, lift, query, *nets)
+    )(active, cells, pts, lift, query, *nets)
 
 
 def level_kernel(
-    order_ref, count_ref, edge_ref, cells_ref, own_ref, left_ref, right_ref, grad_ref, kept_ref,
+    active_ref, edge_ref, cells_ref, own_ref, left_ref, right_ref, grad_ref, kept_ref,
     weight_ref, bias_ref, out_w_ref, pred_ref, sg_ref, lz_ref, pre_ref, lat_ref, table_ref, got_ref,
     gp_ref, win_ref, sum_ref,
 ):
@@ -178,7 +184,7 @@
         lat_ref[0:channels, x * PLANE : (x + 1) * PLANE] = out
         lat_ref[channels:, x * PLANE : (x + 1) * PLANE] = pltpu.roll(out, PLANE - 1, 1)
     for row in range((GXD + 1) * GY):
-        flat = jnp.transpose(lat_ref[:, row * GZ : (row + 1) * GZ], (1, 0))
+        flat = jnp.transpose(lat_ref[:, row * GZ : (row + 1) * GZ].astype(BF), (1, 0)).astype(F32)
         for t in range(4):
             target = row - (t // 2) * GY - t % 2
             if 0 <= target < GXD * GY:
@@ -187,9 +193,10 @@
     pred_ref[...] = jnp.zeros_like(pred_ref)
     out_w = jnp.concatenate([out_w_ref[...], out_w_ref[...]], axis=1).astype(BF)
 
-    @pl.loop(0, count_ref[0])
-    def _(index):
-        slot = order_ref[index]
+    @pl.loop(0, active_ref.shape[0])
+    def _(slot):
+      @pl.when(active_ref[slot] > 0)
+      def _():
 
         @pl.loop(0, 128 // UNROLL)
         def _(group):
@@ -199,7 +206,7 @@
 
         queried = None
         for t in range(4):
-            term = got_ref[:, t, :] * kept_ref[index, t].astype(F32)
+            term = got_ref[:, t, :] * kept_ref[slot, t].astype(F32)
             queried = term if queried is None else queried + term
         pred_ref[slot] = lax.dot_general(out_w, queried.astype(BF), NT, preferred_element_type=F32)
 
@@ -227,7 +234,7 @@
         ].astype(BF)
 
 
-def level(order, count, edge, cells, own, left, right, grad, kept, weight, bias, out_w):
+def level(active, edge, cells, own, left, right, grad, kept, weight, bias, out_w):
     channels = own.shape[0]
     slots = cells.shape[0]
     smem = pl.BlockSpec(memory_space=pltpu.SMEM)
@@ -238,7 +245,7 @@
             jax.ShapeDtypeStruct((slots, out_w.shape[0], 128), F32),
             jax.ShapeDtypeStruct((channels, 27 * channels), BF),
         ],
-        in_specs=[smem] * 4 + [vmem] * 8,
+        in_specs=[smem] * 3 + [vmem] * 8,
         out_specs=[vmem] * 2,
         scratch_shapes=[
             pltpu.VMEM((3 * channels, 5 * PADDED), BF),
@@ -251,7 +258,63 @@
             pltpu.VMEM((3 * channels, 9 * channels), F32),
         ],
         compiler_params=pltpu.CompilerParams(vmem_limit_bytes=VMEM_LIMIT),
-    )(order, count, edge, cells, own, left, right, grad, kept, weight, bias, out_w)
+    )(active, edge, cells, own, left, right, grad, kept, weight, bias, out_w)
+
+
+def exchange_kernel(devices, src_ref, out_ref, send_sem, recv_sem, own_sem):
+    me = lax.axis_index("gx")
+    barrier = pltpu.get_barrier_semaphore()
+
+    def greet(d, carry):
+        pl.semaphore_signal(
+            barrier, inc=1, device_id={"gx": lax.rem(me + d, devices)}, device_id_type=pl.DeviceIdType.MESH
+        )
+        return carry
+
+    lax.fori_loop(1, devices, greet, 0)
+    pl.semaphore_wait(barrier, devices - 1)
+    own = pltpu.make_async_copy(src_ref.at[me], out_ref.at[me], own_sem)
+    own.start()
+
+    def sending(d):
+        peer = lax.rem(me + d, devices)
+        return pltpu.make_async_remote_copy(
+            src_ref=src_ref.at[peer],
+            dst_ref=out_ref.at[me],
+            send_sem=send_sem.at[d],
+            recv_sem=recv_sem.at[d],
+            device_id={"gx": peer},
+            device_id_type=pl.DeviceIdType.MESH,
+        )
+
+    def start(d, carry):
+        sending(d).start()
+        return carry
+
+    def finish(d, carry):
+        sending(d).wait()
+        return carry
+
+    lax.fori_loop(1, devices, start, 0)
+    own.wait()
+    lax.fori_loop(1, devices, finish, 0)
+
+
+def exchange(blocks, collective_id):
+    devices = blocks.shape[0]
+    vmem = pl.BlockSpec(memory_space=pltpu.VMEM)
+    return pl.pallas_call(
+        functools.partial(exchange_kernel, devices),
+        out_shape=jax.ShapeDtypeStruct(blocks.shape, blocks.dtype),
+        in_specs=[vmem],
+        out_specs=vmem,
+        scratch_shapes=[
+            pltpu.SemaphoreType.DMA((devices,)),
+            pltpu.SemaphoreType.DMA((devices,)),
+            pltpu.SemaphoreType.DMA,
+        ],
+        compiler_params=pltpu.CompilerParams(collective_id=collective_id, has_side_effects=True),
+    )(blocks)
 
 
 def shards(
@@ -281,30 +344,21 @@
             (base_cell % GZ).astype(BF)[:, None],
             corner_bits.astype(BF)[:, None],
             jnp.ones((held, 1, 128), BF),
-            jnp.zeros((held, 4, 128), BF),
+            jnp.zeros((held, 12, 128), BF),
         ],
         axis=1,
     ).reshape(held, -1)
     sent = jnp.dot(pick.T, packed, preferred_element_type=F32).astype(BF)
-    pts = lax.all_to_all(sent, "gx", split_axis=0, concat_axis=0, tiled=True)
-    pts = pts.reshape(slots, 24, 128).astype(F32)
-
-    active = pts[:, 19, 0] > 0.5
-    before = jnp.arange(slots)[None, :] < jnp.arange(slots)[:, None]
-    count = jnp.sum(active.astype(jnp.int32))
-    ahead_on = jnp.sum((before & active[None, :]).astype(jnp.int32), axis=1)
-    ahead_off = jnp.sum((before & ~active[None, :]).astype(jnp.int32), axis=1)
-    place = jnp.where(active, ahead_on, count + ahead_off)
-    order = jnp.sum(
-        jnp.where(place[None, :] == jnp.arange(slots)[:, None], jnp.arange(slots)[None, :], 0), axis=1
-    ).astype(jnp.int32)
-    count = count.reshape(1)
+    pts = exchange(sent.reshape(devices, CAP * 32, 128), 0)
+    pts = pts.reshape(slots, 32, 128)[:, :24].astype(F32)
+
+    active = pts[:, 19, 0].astype(jnp.int32)
     edge = (me == devices - 1).astype(jnp.int32).reshape(1)
 
     cells = (pts[:, 16] * GZ + pts[:, 17]).astype(jnp.int32)
     query = jnp.pad(output_weight.astype(F32), ((0, 4), (0, 0)))
     own, grad, kept = scatter_points(
-        order, count, cells, pts, lift_weight.astype(F32).T, query,
+        active, cells, pts, lift_weight.astype(F32).T, query,
         encode_inner.T, encode_bias[None], encode_outer, decode_inner.T, decode_bias[None], decode_outer,
     )
     up = [(i, i + 1) for i in range(devices - 1)]
@@ -317,12 +371,14 @@
         .reshape(9 * channels, 3 * channels)
     )
     predicted, terms = level(
-        order, count, edge, cells, own, left, right, grad, kept, weight, stencil_bias[:, None], query
+        active, edge, cells, own, left, right, grad, kept, weight, stencil_bias[:, None], query
     )
     outc = output_weight.shape[0]
     predicted = predicted[:, :outc].astype(BF).reshape(devices, -1)
     payload = jnp.concatenate([predicted, terms.reshape(devices, -1)], axis=1)
-    back = lax.all_to_all(payload, "gx", split_axis=0, concat_axis=0, tiled=True)
+    width = payload.shape[1]
+    payload = jnp.pad(payload, ((0, 0), (0, -width % 2048)))
+    back = exchange(payload.reshape(devices, -1, 128), 1).reshape(devices, -1)[:, :width]
     split = CAP * outc * 128
     returned = back[:, :split].reshape(slots, outc * 128)
     answer = jnp.dot(pick, returned, preferred_element_type=F32).astype(BF).reshape(held, outc, 128)

time: 151 us -> 149 us (0.987); the launches traced: 151 us -> 146 us
  Pallas kernels: 58.6 us -> 119 us
  blocking collectives: 51.1 us -> 0 us
  starting transfers between devices: 11.7 us -> 4.36 us
  waiting for transfers between devices: 6.45 us -> 0.01 us
  local copies, waits for them, and re-layouts: 12 us -> 15.1 us
  other arithmetic: 9.75 us -> 6.93 us
    pallas_call x0 -> x2, Pallas kernels: none -> 60.1 us  [exchange(): pl.pallas_call(functools.partial(exchange_kernel, devices), out_shape=jax...]
    all_to_all x1 -> x0, blocking collectives: 51.1 us -> none  [shards(): lax.all_to_all(payload, 'gx', split_axis=0, concat_axis=0, tiled=True)]
    all_to_all x1 -> x0, starting transfers between devices: 7.39 us -> none  [shards(): pts = lax.all_to_all(sent, 'gx', split_axis=0, concat_axis=0, tiled=True)]
    all_to_all x1 -> x0, waiting for transfers between devices: 6.45 us -> none  [shards(): pts = lax.all_to_all(sent, 'gx', split_axis=0, concat_axis=0, tiled=True)]
    unnamed x14 -> x11, local copies, waits for them, and re-layouts: 2.05 us -> 3.58 us
  transfers between devices with their start and end apart: 3 -> 2, of which waited for: 1 -> 0; matrix products, arithmetic and copies ran while one was open for 3% -> 1% of each run, Pallas kernels for 0% -> 0%
where the time goes in v3:
time: 149 us; the launch traced here: 146 us
  Pallas kernels  119 us (80%)
  local copies, waits for them, and re-layouts  15.1 us (10%)
  other arithmetic  6.93 us (5%)
  starting transfers between devices  4.36 us (3%)
    pallas_call x2, Pallas kernels, exchange(): pl.pallas_call(functools.partial(exchange_kernel, devices), out_shape=jax...  60.1 us
    pallas_call x1, Pallas kernels, scatter_points(): pl.pallas_call(scatter_kernel, out_shape=[jax.ShapeDtypeStruct((channels,...  35.4 us
    pallas_call x1, Pallas kernels, level(): pl.pallas_call(level_kernel, out_shape=[jax.ShapeDtypeStruct((slots, out_...  23.1 us
    unnamed x11, local copies, waits for them, and re-layouts  3.58 us
    ppermute x1, starting transfers between devices, shards(): left = lax.ppermute(own[:, PLANE:], 'gx', up)  3.06 us
  transfers between devices with their start and end apart: 2, of which 0 were waited for; matrix products, arithmetic and copies ran while one was open for 1% of the time, Pallas kernels for 0%

profile of v3, /device:TPU:0, one launch (start us, length us, event | category | flops | bytes accessed | tf_op | source)
XLA Modules:
  0.0 146.4 jit_solution(8164815741150623803)
XLA Ops:
  0.6 0.9 convert_reduce_fusion.1
  1.6 0.7 fusion.18
  2.2 0.7 convert_bitcast_fusion.1
  2.9 0.7 fusion.16
  3.7 0.7 copy.33
  4.4 1.8 %concatenate.6 = bf16[16,32,128]{2,1,0:T(8,128)(2,1)S(1)} concatenate(bf16[16,8,128]{2,1,0:T(8,128)(2,1)} %param.17, bf16[16,4,128]{2,1,0:T(4,128)(2,1)} %param.21, bf16[16,3,128]{2,1,0:T(4,128)(2,1)S(1)} %copy.33, bf16[16,1,128]{2,1,0:T(2,128)(2,1)S(1)} %broadcast_in_dim.31, bf16[16,1,128]{2,1,0:T(2,128)(2,1)S(1)} %copy.34, bf16[16,1,128]{2,1,0:T(2,128)(2,1)S(1)} %copy.35, ...), dimensions={1} | concatenate | bytes 262144 | tf_op jit(solution)/shard_map/concatenate | solution.py:337
  6.3 0.3 convolution_convert_fusion
  6.6 0.8 reshape.53.src_ref
  7.4 12.8 %shard_map.167 = bf16[16,64,128]{2,1,0:T(8,128)(2,1)} custom-call(bf16[16,64,128]{2,1,0:T(8,128)(2,1)} %reshape.53.src_ref), custom_call_target="tpu_custom_call" | custom-call | tf_op jit(solution)/shard_map/pallas_call | solution.py:306
  20.2 1.0 slice.40
  21.2 0.7 fusion.8.active_ref
  21.8 0.6 fusion.7.cells_ref
  22.4 1.0 copy.38.pts_ref
  23.4 1.3 pad_convert_fusion.query_ref.out_w_ref
  24.7 1.3 convert_bitcast_fusion.lift_ref
  26.0 35.4 %shard_map.168 = (bf16[64,6144]{1,0:T(8,128)(2,1)}, f32[64,6144]{1,0:T(8,128)}, bf16[32,4,128,128]{3,2,1,0:T(8,128)(2,1)}) custom-call(s32[32]{0:T(128)} %fusion.8.active_ref, s32[32,128]{1,0:T(8,128)} %fusion.7.cells_ref, f32[32,24,128]{2,1,0:T(8,128)} %copy.38.pts_ref, f32[8,64]{1,0:T(8,128)} %convert_bitcast_fusion.lift_ref, ...), custom_call_target="tpu_custom_call" | custom-call | tf_op jit(solution)/shard_map/pallas_call | solution.py:121
  61.4 1.3 fusion.19
  62.6 1.3 collective-permute-start.1
  63.9 3.1 %collective-permute-start = (bf16[64,4096]{1,0:T(8,128)(2,1)S(1)}, bf16[64,4096]{1,0:T(8,128)(2,1)S(1)}, u32[]{:S(2)}, u32[]{:S(2)}) collective-permute-start(bf16[64,4096]{1,0:T(8,128)(2,1)S(1)} %get-tuple-element.13), channel_id=1, source_target_pairs={{0,1},{1,2},{2,3},{3,4},{4,5},{5,6},{6,7},{7,8},{8,9},{9,10},{10,1... | collective-permute-start | bytes 1572872 | tf_op jit(solution)/shard_map/ppermute | solution.py:366
  67.0 0.7 copy.40.bias_ref
  67.7 0.4 copy.52
  68.1 1.1 reshape.58.weight_ref
  69.2 0.8 copy-done
  70.0 0.2 copy-done.1
  70.2 23.1 %shard_map.169 = (f32[32,8,128]{2,1,0:T(8,128)}, bf16[64,1728]{1,0:T(8,128)(2,1)}) custom-call(s32[32]{0:T(128)} %fusion.8.active_ref, s32[1]{0:T(128)} %bitcast.7.edge_ref, s32[32,128]{1,0:T(8,128)} %fusion.7.cells_ref, bf16[64,6144]{1,0:T(8,128)(2,1)} %get-tuple-element.7.own_ref, bf16[64,4096]{1,0:T(8,128)(2,1)} %copy-done.1, bf16[64,4096]{1,0:T(8,128)(2,1)} %copy-done, ...), custom_call_target="tpu_custom_call" | custom-call | tf_op jit(solution)/shard_map/pallas_call | solution.py:242
  93.3 0.9 slice.60
  94.3 1.2 reshape.60
  95.5 0.7 copy.43
  96.2 47.4 %shard_map.170 = bf16[16,64,128]{2,1,0:T(8,128)(2,1)} custom-call(bf16[16,64,128]{2,1,0:T(8,128)(2,1)} %bitcast.41), custom_call_target="tpu_custom_call" | custom-call | tf_op jit(solution)/shard_map/pallas_call | solution.py:306
  143.6 1.1 copy.53
  145.0 0.6 reshape.64
  145.7 0.7 reshape.65
  (21 shorter events, 0.4 us)
Async XLA Ops:
  0.6 66.4 %copy-start.3 = (f32[64]{0:T(128)S(1)}, f32[64]{0:T(128)}, u32[]{:S(2)}) copy-start(f32[64]{0:T(128)} %param.27) | copy-start | bytes 772
  0.6 67.1 %copy-start.2 = (bf16[27,64,64]{2,1,0:T(8,128)(2,1)S(1)}, bf16[27,64,64]{2,1,0:T(8,128)(2,1)}, u32[]{:S(2)}) copy-start(bf16[27,64,64]{2,1,0:T(8,128)(2,1)} %param.26) | copy-start | bytes 663556
  62.6 6.5 %collective-permute-start.1 = (bf16[64,4096]{1,0:T(8,128)(2,1)S(1)}, bf16[64,4096]{1,0:T(8,128)(2,1)S(1)}, u32[]{:S(2)}, u32[]{:S(2)}) collective-permute-start(bf16[64,4096]{1,0:T(8,128)(2,1)S(1)} %get-tuple-element.12), channel_id=1, source_target_pairs={{1,0},{2,1},{3,2},{4,3},{5,4},{6,5},{7,6},{8,7},{9,8},{10,9},{11,1... | collective-permute-start | bytes 1572872 | tf_op jit(solution)/shard_map/ppermute | solution.py:367
  63.9 5.2 %collective-permute-start = (bf16[64,4096]{1,0:T(8,128)(2,1)S(1)}, bf16[64,4096]{1,0:T(8,128)(2,1)S(1)}, u32[]{:S(2)}, u32[]{:S(2)}) collective-permute-start(bf16[64,4096]{1,0:T(8,128)(2,1)S(1)} %get-tuple-element.13), channel_id=1, source_target_pairs={{0,1},{1,2},{2,3},{3,4},{4,5},{5,6},{6,7},{7,8},{8,9},{9,10},{10,1... | collective-permute-start | bytes 1572872 | tf_op jit(solution)/shard_map/ppermute | solution.py:366
  69.2 0.8 copy-start
  69.2 1.0 copy-start.1
